TPU v7x, 256 devices: a whole 4x4x8 slice. The times are simulated.
256 devices in a mesh: tile: 16 (over z, core), depth: 16 (over y, x).
Axes of the slice: x: 4, y: 4, z: 8, core: 2. Of those that a mesh axis runs over, the one named last changes fastest.
Arguments:
- volume: bfloat16 [1024, 256, 4096], P('depth', 'tile'), may hold values from 0 to 1
- tf_color: float32 [3, 16], replicated, may hold values from 0 to 1
- tf_opacity: float32 [16], replicated, may hold values from 0.0003 to 0.06
- light: float32 [3], replicated, may hold values from -3 to 3
- background: float32 [3], replicated, may hold values from 0 to 1
- exposure_prior: float32 [1], replicated, may hold values from 0.5 to 4
Outputs:
- mapped: float32 [2, 3, 256, 4096], P(None, None, 'tile', 'depth')
All inputs are finite; a program needn't handle non-finite values.
Results may differ from a plain program's by a relative error of at most 0.00045.
Values may be sent and summed in bfloat16 or wider, within the bound.
No kernel may reach another device: no remote copies, remote signals or barrier semaphores. Data moves between devices by JAX's collectives and lax.ppermute only.
A program may use at most 128 MiB of HBM per device.

v0:
```python
import math

import jax
import jax.numpy as jnp
from jax import lax
from jax.sharding import PartitionSpec as P

BINS = 64


AMBIENT = 0.3
GRAD_FLOOR = 0.04
REF_DEPTH = 1024.0
LUMA_EPS = 0.01
LOG_LOW = math.log(0.01)
LOG_HIGH = 0.05
EXPOSURE_KEY = 0.25


def padded_2(block, sides, width):
    for axis, dim in sides:
        count = lax.axis_size(axis)
        forward = [(i, i + 1) for i in range(count - 1)]
        backward = [(target, source) for source, target in forward]
        low = lax.ppermute(
            lax.slice_in_dim(block, block.shape[dim] - width, None, axis=dim), axis, forward
        )
        high = lax.ppermute(lax.slice_in_dim(block, 0, width, axis=dim), axis, backward)
        block = jnp.concatenate([low, block, high], axis=dim)
    return block


def sample_plane(below, centre_rows, above, tf_color, tf_opacity, light, step_len):
    centre = centre_rows[1:-1]
    grad_depth = 0.5 * (above[1:-1] - below[1:-1])
    grad_rows = 0.5 * (centre_rows[2:] - centre_rows[:-2])
    sided = jnp.pad(centre, ((0, 0), (1, 1)))
    grad_cols = 0.5 * (sided[:, 2:] - sided[:, :-2])
    length = jnp.sqrt(
        grad_depth * grad_depth + grad_rows * grad_rows + grad_cols * grad_cols + GRAD_FLOOR
    )
    light_len = jnp.sqrt(jnp.sum(light * light) + 1.0)
    facing = (grad_depth * light[0] + grad_rows * light[1] + grad_cols * light[2]) / (
        length * light_len
    )
    shade = AMBIENT + (1.0 - AMBIENT) * (0.5 + 0.5 * facing)
    knot_count = tf_color.shape[1]
    scaled = centre * (knot_count - 1)
    colour = jnp.zeros((3,) + centre.shape, jnp.float32)
    opacity = jnp.zeros(centre.shape, jnp.float32)
    for knot in range(knot_count):
        weight = jnp.maximum(0.0, 1.0 - jnp.abs(scaled - knot))
        colour = colour + weight[None] * tf_color[:, knot][:, None, None]
        opacity = opacity + weight * tf_opacity[knot]
    return (colour * shade[None], opacity * step_len)


def march_step(state, colour, alpha):
    front_image, back_image = state
    sample = jnp.concatenate([colour * alpha[None], alpha[None]], 0)
    front_image = front_image + (1.0 - front_image[3:4]) * sample
    back_image = sample + (1.0 - alpha[None]) * back_image
    return (front_image, back_image)


def place_over(front, back):
    return front + (1.0 - front[3:4]) * back


def ordered(lower, higher, modes):
    blended = []
    for view_index in range(len(modes)):
        if modes[view_index] == "forward":
            blended.append(place_over(lower[view_index], higher[view_index]))
        else:
            blended.append(place_over(higher[view_index], lower[view_index]))
    return jnp.stack(blended)


def composite(partial_value, modes):
    stack = lax.all_to_all(partial_value[None], "depth", split_axis=4, concat_axis=0, tiled=True)

    def fold_layer(running, layer):
        return (ordered(running, layer, modes), None)

    running, unused = lax.scan(fold_layer, jnp.zeros_like(stack[0]), stack)
    return running


def flatten(final, background):
    return final[:3] + (1.0 - final[3:4]) * background[:, None, None]


def luma_log(colour_rgb):
    return jnp.log(
        0.2126 * colour_rgb[0] + 0.7152 * colour_rgb[1] + 0.0722 * colour_rgb[2] + LUMA_EPS
    )


def bin_centres(count):
    return LOG_LOW + jnp.arange(count, dtype=jnp.float32) * ((LOG_HIGH - LOG_LOW) / (count - 1))


def global_histogram(first_rgb):
    bin_width = (LOG_HIGH - LOG_LOW) / (BINS - 1)
    centres = bin_centres(BINS)
    log_luma = luma_log(first_rgb)
    totals = []
    for index in range(BINS):
        totals.append(
            jnp.sum(jnp.maximum(0.0, 1.0 - jnp.abs(log_luma - centres[index]) / bin_width))
        )
    return lax.psum(jnp.stack(totals), ("tile", "depth"))


def tone(colour_rgb, exposure):
    scaled = exposure * colour_rgb
    return scaled / (1.0 + scaled)


def local(volume, tf_color, tf_opacity, light, background, exposure_prior):
    slab = volume.shape[0]
    row_count = volume.shape[1]
    width_count = volume.shape[2]
    step_len = REF_DEPTH / (slab * lax.axis_size("depth"))
    padded = padded_2(volume, (("depth", 0), ("tile", 1)), 1)

    def advance(state, plane_index):
        below = lax.dynamic_index_in_dim(padded, plane_index, 0, keepdims=False).astype(jnp.float32)
        here = lax.dynamic_index_in_dim(padded, plane_index + 1, 0, keepdims=False).astype(
            jnp.float32
        )
        above = lax.dynamic_index_in_dim(padded, plane_index + 2, 0, keepdims=False).astype(
            jnp.float32
        )
        colour, alpha = sample_plane(below, here, above, tf_color, tf_opacity, light, step_len)
        return (march_step(state, colour, alpha), None)

    empty = jnp.zeros((4, row_count, width_count), jnp.float32)
    (front_image, back_image), unused = lax.scan(
        advance, (empty, empty), jnp.arange(slab, dtype=jnp.int32)
    )
    partial_value = jnp.stack([front_image, back_image])
    images = composite(partial_value, ("forward", "backward"))
    first_rgb = flatten(images[0], background)
    counts = global_histogram(first_rgb)
    second_rgb = flatten(images[1], background)
    pixel_total = row_count * lax.axis_size("tile") * width_count
    mean_log = jnp.sum(counts * bin_centres(BINS)) / pixel_total
    exposure_next = EXPOSURE_KEY * jnp.exp(-mean_log)
    return jnp.stack([tone(first_rgb, exposure_prior[0]), tone(second_rgb, exposure_next)])


def solution(mesh):
    placed = (P("depth", "tile", None), P(), P(), P(), P(), P())
    return jax.shard_map(
        local, mesh=mesh, in_specs=placed, out_specs=P(None, None, "tile", "depth"), check_vma=False
    )
```

profile of v0, /device:TPU:1, one launch (start us, length us, event | category | flops | bytes accessed | tf_op | source)
XLA Modules:
  0.0 1700.3 jit_solution(8498516063559942758)
XLA Ops:
  0.0 11.2 copy.17
  55.4 18.7 %copy.20 = bf16[66,18,4096]{2,1,0:T(8,128)(2,1)} copy(bf16[66,18,4096]{2,0,1:T(8,128)(2,1)S(1)} %pad_maximum_fusion.2) | data formatting | bytes 19464192
  74.1 1332.2 %while.26 = (s32[]{:T(128)}, f32[4,16,4096]{2,1,0:T(8,128)S(1)}, f32[4,16,4096]{2,1,0:T(8,128)S(1)}, s32[64]{0:T(128)S(1)}, bf16[66,18,4096]{2,1,0:T(8,128)(2,1)...) while((s32[]{:T(128)}, f32[4,16,4096]{2,1,0:T(8,128)S(1)}, ...), condition=%wide.region_2.3_spmd.clone, body=%wide.region_1.2_spmd.clone.sunk | while | flops 20848652 | bytes 21415012 | solution.py:140
  81.7 10.7 broadcast_subtract_fusion.2
  102.5 10.7 broadcast_subtract_fusion.2
  123.3 10.7 broadcast_subtract_fusion.2
  144.1 10.7 broadcast_subtract_fusion.2
  164.9 10.7 broadcast_subtract_fusion.2
  185.8 10.7 broadcast_subtract_fusion.2
  206.6 10.7 broadcast_subtract_fusion.2
  227.4 10.7 broadcast_subtract_fusion.2
  248.2 10.7 broadcast_subtract_fusion.2
  269.0 10.7 broadcast_subtract_fusion.2
  289.8 10.7 broadcast_subtract_fusion.2
  310.7 10.7 broadcast_subtract_fusion.2
  331.5 10.7 broadcast_subtract_fusion.2
  352.3 10.7 broadcast_subtract_fusion.2
  373.1 10.7 broadcast_subtract_fusion.2
  393.9 10.7 broadcast_subtract_fusion.2
  414.7 10.7 broadcast_subtract_fusion.2
  435.6 10.7 broadcast_subtract_fusion.2
  477.2 10.7 broadcast_subtract_fusion.2
  518.8 10.7 broadcast_subtract_fusion.2
  539.6 10.7 broadcast_subtract_fusion.2
  560.4 10.7 broadcast_subtract_fusion.2
  581.3 10.7 broadcast_subtract_fusion.2
  602.1 10.7 broadcast_subtract_fusion.2
  622.9 10.7 broadcast_subtract_fusion.2
  643.7 10.7 broadcast_subtract_fusion.2
  664.5 10.7 broadcast_subtract_fusion.2
  706.2 10.7 broadcast_subtract_fusion.2
  747.8 10.7 broadcast_subtract_fusion.2
  789.4 10.7 broadcast_subtract_fusion.2
  831.1 10.7 broadcast_subtract_fusion.2
  872.7 10.7 broadcast_subtract_fusion.2
  914.3 10.7 broadcast_subtract_fusion.2
  935.1 10.7 broadcast_subtract_fusion.2
  955.9 10.7 broadcast_subtract_fusion.2
  976.8 10.7 broadcast_subtract_fusion.2
  997.6 10.7 broadcast_subtract_fusion.2
  1018.4 10.7 broadcast_subtract_fusion.2
  1039.2 10.7 broadcast_subtract_fusion.2
  1060.0 10.7 broadcast_subtract_fusion.2
  1101.7 10.7 broadcast_subtract_fusion.2
  1143.3 10.7 broadcast_subtract_fusion.2
  1184.9 10.7 broadcast_subtract_fusion.2
  1226.6 10.7 broadcast_subtract_fusion.2
  1268.2 10.7 broadcast_subtract_fusion.2
  1309.8 10.7 broadcast_subtract_fusion.2
  1330.6 10.7 broadcast_subtract_fusion.2
  1351.4 10.7 broadcast_subtract_fusion.2
  1372.3 10.7 broadcast_subtract_fusion.2
  1393.1 10.7 broadcast_subtract_fusion.2
  1407.8 13.0 copy.22
  1420.8 14.5 bitcast_bitcast_fusion
  1435.3 18.8 %reshape.716 = f32[16,1,32768]{2,1,0:T(1,128)} reshape(f32[4096,1,2,4,16]{4,3,2,1,0:T(4,128)} %bitcast_bitcast_fusion) | data formatting | bytes 4194304
  1465.9 21.1 %all-to-all-done = f32[16,1,32768]{2,1,0:T(1,128)S(1)} async-done(((f32[16,1,32768]{2,1,0:T(1,128)}), f32[16,1,32768]{2,1,0:T(1,128)S(1)}, u32[]{:S(2)}, u32[]{:S(2)}) %all-to-all-start) | async-done | bytes 2097184 | tf_op jit(solution)/shard_map/all_to_all | solution.py:81
  1496.2 17.9 %reshape.717 = f32[4096,1,2,4,16]{4,3,2,1,0:T(4,128)} reshape(f32[16,32768]{1,0:T(8,128)S(1)} %reduce.64) | data formatting | bytes 4194304
  1514.1 13.1 copy.23
  1528.9 11.8 maximum_reduce_fusion
  1547.8 12.1 maximum_reduce_fusion.18
  1559.9 11.8 maximum_reduce_fusion.36
  1571.7 41.1 %stack.281 = f32[64]{0:T(128)S(1)} concatenate(f32[1]{0:T(128)} %bitcast.17, f32[1]{0:T(128)} %bitcast.19, f32[1]{0:T(128)} %bitcast.21, f32[1]{0:T(128)} %bitcast.23, f32[1]{0:T(128)} %bitcast.25, f32[1]{0:T(128)} %bitcast.27, f32[1]{0:T(128)} %bitcast.29, f32[1]{0:T(128)} %bitcast.31, f32[1]{0:T(128)} %bitcast.33, f32[1]{0:T(128)} %bitcast.35, f32[1]{0:T(128)} %bitcast.37, ...), dimensions={0} | concatenate | bytes 512 | tf_op jit(solution)/shard_map/stack | solution.py:113
  1612.8 85.4 %psum.7 = f32[64]{0:T(128)S(1)} all-reduce(f32[64]{0:T(128)S(1)} %stack.281), channel_id=1, replica_groups=mesh['tile'=16,'depth'=16] {'tile','depth'}, use_global_device_ids=true, to_apply=%region_69.70 | all-reduce | flops 64 | bytes 512 | tf_op jit(solution)/shard_map/psum | solution.py:113
  (826 shorter events, 616.6 us)
Async XLA Ops:
  11.2 24.8 %copy-start.2 = (f32[3]{0:T(128)S(1)}, f32[3]{0:T(128)}, u32[]{:S(2)}) copy-start(f32[3]{0:T(128)} %param.13) | copy-start | bytes 40
  11.2 27.5 %copy-start.4 = (f32[3,16]{1,0:T(4,128)S(1)}, f32[3,16]{1,0:T(4,128)}, u32[]{:S(2)}) copy-start(f32[3,16]{1,0:T(4,128)} %param.11) | copy-start | bytes 580
  13.3 8.9 collective-permute-start
  17.3 8.8 collective-permute-start.1
  28.6 12.4 collective-permute-start.2
  33.9 11.5 collective-permute-start.3
  55.4 18.7 %copy-start.1 = (f32[16]{0:T(128)S(1)}, f32[16]{0:T(128)}, u32[]{:S(2)}) copy-start(f32[16]{0:T(128)} %param.12) | copy-start | bytes 196
  1454.1 33.0 %all-to-all-start = ((f32[16,1,32768]{2,1,0:T(1,128)}), f32[16,1,32768]{2,1,0:T(1,128)S(1)}, u32[]{:S(2)}, u32[]{:S(2)}) async-start(f32[16,1,32768]{2,1,0:T(1,128)} %reshape.716), calls=%async_computation | async-start | bytes 4194304 | tf_op jit(solution)/shard_map/all_to_all | solution.py:81
  1487.0 1.4 copy-start
  1514.1 14.7 copy-start.3
where the time goes:
time: 1720 us; the launch traced here: 1700 us
  other arithmetic  1060 us (62%)
  loops' own time  257 us (15%)
  local copies, waits for them, and re-layouts  241 us (14%)
  blocking collectives  85.4 us (5%)
  waiting for transfers between devices  34 us (2%)
  starting transfers between devices  20.9 us (1%)
    sub x64, other arithmetic, march_step(): back_image = sample + (1.0 - alpha[None]) * back_image  683 us
    another operation x1, loops' own time, local(): lax.scan(advance, (empty, empty), jnp.arange(slab, dtype=jnp.int32))  256 us
    add x64, other arithmetic, sample_plane(): shade = AMBIENT + (1.0 - AMBIENT) * (0.5 + 0.5 * facing)  90.7 us
    psum x1, blocking collectives, global_histogram(): return lax.psum(jnp.stack(totals), ('tile', 'depth'))  85.4 us
    unnamed x16, local copies, waits for them, and re-layouts  82.5 us
    convert_element_type x64, other arithmetic, advance(): lax.dynamic_index_in_dim(padded, plane_index + 1, 0, keepdims=False)  61.3 us
    mul x64, other arithmetic, march_step(): sample = jnp.concatenate([colour * alpha[None], alpha[None]], 0)  60.8 us
    add x64, other arithmetic, march_step(): back_image = sample + (1.0 - alpha[None]) * back_image  45.8 us
  transfers between devices with their start and end apart: 5, of which 5 were waited for; matrix products, arithmetic and copies ran while one was open for 0% of the time, Pallas kernels for 0%

commit v1 on v0

v1 whole, which is shorter than its diff:
```python
import functools
import math

import jax
import jax.numpy as jnp
import numpy as np
from jax import lax
from jax.experimental import pallas as pl
from jax.experimental.pallas import tpu as pltpu
from jax.sharding import PartitionSpec as P

f32 = jnp.float32
bf16 = jnp.bfloat16

BINS = 64
AMBIENT = 0.3
LUMA_EPS = 0.01
LOG_LOW = math.log(0.01)
LOG_HIGH = 0.05
EXPOSURE_KEY = 0.25
BIN_WIDTH = (LOG_HIGH - LOG_LOW) / (BINS - 1)

PLANES = 64
ROWS = 16
LANES = 128
DEPTH = 16
BLOCKS = 32
CHUNKS = 2
VMEM = 40 * 1024 * 1024


def segment_tables(tf_color, tf_opacity):
    f = jnp.concatenate([tf_opacity[None], tf_color], 0)
    f = jnp.concatenate([f, f[:, 15:]], 1)
    lo, mid, hi = f[:, 0:16:2], f[:, 1:16:2], f[:, 2:17:2]
    centre = (2.0 * jnp.arange(8, dtype=f32) + 1.0)[None]
    t = jnp.concatenate([mid, 0.5 * (hi - lo), 0.5 * (hi + lo) - mid, centre], 0)
    return jnp.broadcast_to(t.reshape(104, 1), (104, LANES))


def difference_matrices():
    sx = np.zeros((3, 384, LANES), np.float32)
    for variant in range(3):
        for i in range(LANES):
            if not (variant == 0 and i == 0):
                sx[variant, LANES + i - 1, i] = -1
            if not (variant == 2 and i == LANES - 1):
                sx[variant, LANES + i + 1, i] = 1
    sy = np.zeros((256, 384), np.float32)
    for p in range(16):
        for r in range(16):
            o = 16 * p + r
            sy[o, o - 1 if r > 0 else 256 + p] = -1
            sy[o, o + 1 if r < 15 else 272 + p] = 1
    return jnp.asarray(sx, bf16), jnp.asarray(sy, bf16)


def pick(table, index):
    return jnp.take_along_axis(table, index, axis=0, mode="promise_in_bounds")


def halves(x):
    x = x.astype(f32)
    return [x[0:8], x[8:16]]


def march_kernel(
    lp_ref, t_ref, sx_ref, sy_ref, vp_ref, v_ref, vn_ref, zlo_ref, zhi_ref, ylo_ref, yhi_ref,
    o_ref, dx_scr, dy_scr,
):
    lz, ly, lx = lp_ref[0], lp_ref[1], lp_ref[2]
    for g in range(4):
        s = slice(16 * g, 16 * g + 16)
        o = slice(256 * g, 256 * g + 256)
        wide = jnp.concatenate([r[s].reshape(256, LANES) for r in (vp_ref, v_ref, vn_ref)], axis=1)
        dx_scr[o] = jnp.dot(wide, sx_ref[0], preferred_element_type=f32)
        tall = jnp.concatenate(
            [v_ref[s].reshape(256, LANES), ylo_ref[s], yhi_ref[s], jnp.zeros((96, LANES), bf16)],
            axis=0,
        )
        dy_scr[o] = jnp.dot(sy_ref[...], tall, preferred_element_type=f32)
    tb = [t_ref[8 * k : 8 * k + 8, :] for k in range(13)]

    def plane(z, carry, above):
        below, here, front, through, back = carry
        new_front, new_through, new_back = [], [], []
        for h in range(2):
            v = here[h]
            rows = pl.ds(pl.multiple_of(16 * z + 8 * h, 8), 8)
            dz = above[h] - below[h]
            dx = dx_scr[rows, :]
            dy = dy_scr[rows, :]
            q = (dz * dz + 0.16) + (dy * dy + dx * dx)
            dot = (dz * lz + dy * ly) + dx * lx
            shade = 0.65 + dot * lax.rsqrt(q)
            j = (v * 7.5).astype(jnp.int32)
            u = v * 15.0 - pick(tb[12], j)
            au = jnp.abs(u)
            alpha, red, green, blue = [
                pick(tb[k], j) + pick(tb[4 + k], j) * u + pick(tb[8 + k], j) * au for k in range(4)
            ]
            w = alpha * shade
            keep = 1.0 - alpha
            p = [w * c for c in (red, green, blue)]
            new_front.append([front[h][i] + through[h] * p[i] for i in range(3)])
            new_back.append([back[h][i] * keep + p[i] for i in range(3)])
            new_through.append(through[h] * keep)
        return (here, above, new_front, new_through, new_back)

    zero = jnp.zeros((8, LANES), f32)
    one = jnp.ones((8, LANES), f32)
    carry = (halves(zlo_ref[...]), halves(v_ref[0]), [[zero] * 3] * 2, [one] * 2, [[zero] * 3] * 2)
    carry = lax.fori_loop(
        0, PLANES - 1, lambda z, c: plane(z, c, halves(v_ref[z + 1])), carry, unroll=3
    )
    carry = plane(PLANES - 1, carry, halves(zhi_ref[...]))
    _, _, front, through, back = carry
    for h in range(2):
        s = slice(8 * h, 8 * h + 8)
        for i in range(3):
            o_ref[0, i, s] = front[h][i]
            o_ref[0, 4 + i, s] = back[h][i]
        o_ref[0, 3, s] = through[h]


def march(chunk, vol, zlo, zhi, ylo, yhi, lp, tab, sx, sy):
    def block(shift):
        return pl.BlockSpec(
            (PLANES, ROWS, LANES), lambda d: (0, 0, jnp.clip(2 * d + chunk + shift, 0, BLOCKS - 1))
        )

    def edge(n):
        return pl.BlockSpec((n, LANES), lambda d: (0, 2 * d + chunk))

    def variant(d):
        at = 2 * d + chunk
        return (jnp.where(at == 0, 0, jnp.where(at == BLOCKS - 1, 2, 1)), 0, 0)

    return pl.pallas_call(
        march_kernel,
        grid=(DEPTH,),
        in_specs=[
            pl.BlockSpec(memory_space=pltpu.SMEM),
            pl.BlockSpec(tab.shape, lambda d: (0, 0)),
            pl.BlockSpec((1, 384, LANES), variant),
            pl.BlockSpec(sy.shape, lambda d: (0, 0)),
            block(-1),
            block(0),
            block(1),
            edge(ROWS),
            edge(ROWS),
            edge(PLANES),
            edge(PLANES),
        ],
        out_specs=pl.BlockSpec((1, 7, ROWS, LANES), lambda d: (d, 0, 0, 0)),
        out_shape=jax.ShapeDtypeStruct((DEPTH, 7, ROWS, LANES), f32),
        scratch_shapes=[pltpu.VMEM((1024, LANES), f32), pltpu.VMEM((1024, LANES), f32)],
        compiler_params=pltpu.CompilerParams(vmem_limit_bytes=VMEM),
        cost_estimate=pl.CostEstimate(
            flops=200_000_000, bytes_accessed=12_000_000, transcendentals=2_000_000
        ),
        name="march",
    )(lp, tab, sx, sy, vol, vol, vol, zlo, zhi, ylo, yhi)


def composite_kernel(bg_ref, prior_ref, s0_ref, s1_ref, mapped_ref, second_ref, lum_ref):
    total = jnp.zeros((8, LANES), f32)
    for c, s_ref in enumerate((s0_ref, s1_ref)):
        cols = slice(LANES * c, LANES * c + LANES)
        through = s_ref[0, 3]
        front = [s_ref[0, i] for i in range(3)]
        back = [s_ref[0, 4 + i] for i in range(3)]
        for d in range(1, DEPTH):
            t = s_ref[d, 3]
            front = [front[i] + through * s_ref[d, i] for i in range(3)]
            back = [s_ref[d, 4 + i] + t * back[i] for i in range(3)]
            through = through * t
        front = [front[i] + through * bg_ref[i] for i in range(3)]
        back = [back[i] + through * bg_ref[i] for i in range(3)]
        lum = jnp.log(0.2126 * front[0] + 0.7152 * front[1] + 0.0722 * front[2] + LUMA_EPS)
        near = jnp.clip(lum, LOG_LOW, LOG_HIGH)
        term = near * jnp.maximum(0.0, 1.0 - jnp.abs(lum - near) * (1.0 / BIN_WIDTH))
        total = total + term[0:8] + term[8:16]
        for i in range(3):
            scaled = prior_ref[0] * front[i]
            mapped_ref[i, :, cols] = scaled / (1.0 + scaled)
            second_ref[i, :, cols] = back[i]
    lum_ref[...] = jnp.sum(total, axis=0, keepdims=True)


def finish_kernel(pixels, lum_ref, mapped_ref, second_ref, o_ref):
    mean = jnp.sum(lum_ref[...], axis=(0, 1), keepdims=True) / pixels
    exposure = EXPOSURE_KEY * jnp.exp(-mean)
    for i in range(3):
        o_ref[0, i] = mapped_ref[i]
        scaled = exposure * second_ref[i]
        o_ref[1, i] = scaled / (1.0 + scaled)


def neighbours(low_source, high_source, axis):
    count = lax.axis_size(axis)
    forward = [(i, i + 1) for i in range(count - 1)]
    backward = [(target, source) for source, target in forward]
    return lax.ppermute(low_source, axis, forward), lax.ppermute(high_source, axis, backward)


def local(volume, tf_color, tf_opacity, light, background, exposure_prior):
    zlo, zhi = neighbours(volume[PLANES - 1], volume[0], "depth")
    ylo, yhi = neighbours(volume[:, ROWS - 1], volume[:, 0], "tile")
    tab = segment_tables(tf_color, tf_opacity)
    lp = (0.5 * (1.0 - AMBIENT)) * light / jnp.sqrt(jnp.sum(light * light) + 1.0)
    sx, sy = difference_matrices()
    stacks = []
    for chunk in range(CHUNKS):
        part = march(chunk, volume, zlo, zhi, ylo, yhi, lp, tab, sx, sy)
        stacks.append(lax.all_to_all(part, "depth", split_axis=0, concat_axis=0, tiled=True))
    smem = pl.BlockSpec(memory_space=pltpu.SMEM)
    vmem = pl.BlockSpec(memory_space=pltpu.VMEM)
    mapped, second, lum = pl.pallas_call(
        composite_kernel,
        in_specs=[smem, smem, vmem, vmem],
        out_specs=[vmem] * 3,
        out_shape=[
            jax.ShapeDtypeStruct((3, ROWS, 256), f32),
            jax.ShapeDtypeStruct((3, ROWS, 256), f32),
            jax.ShapeDtypeStruct((1, LANES), f32),
        ],
        name="composite",
    )(background, exposure_prior, *stacks)
    sums = lax.all_gather(lum, ("tile", "depth"), axis=0, tiled=True)
    pixels = ROWS * lax.axis_size("tile") * volume.shape[2]
    return pl.pallas_call(
        functools.partial(finish_kernel, float(pixels)),
        in_specs=[vmem] * 3,
        out_specs=vmem,
        out_shape=jax.ShapeDtypeStruct((2, 3, ROWS, 256), f32),
        name="finish",
    )(sums, mapped, second)


def solution(mesh):
    placed = (P("depth", "tile", None), P(), P(), P(), P(), P())
    return jax.shard_map(
        local, mesh=mesh, in_specs=placed, out_specs=P(None, None, "tile", "depth"), check_vma=False
    )
```

time: 1720 us -> 241 us (0.14); the launches traced: 1700 us -> 240 us
  other arithmetic: 1060 us -> 3.42 us
  loops' own time: 257 us -> 0 us
  local copies, waits for them, and re-layouts: 241 us -> 16.9 us
  Pallas kernels: 0 us -> 78.2 us
  waiting for transfers between devices: 34 us -> 14.4 us
    sub x97 -> x0, other arithmetic: 684 us -> none  [the longest x64 683 us: march_step(): back_image = sample + (1.0 - alpha[None]) * back_image]
    another operation x2 -> x0, loops' own time: 257 us -> none  [the longest x1 256 us: local(): lax.scan(advance, (empty, empty), jnp.arange(slab, dtype=jnp.int32))]
    add x146 -> x1, other arithmetic: 137 us -> 0.01 us  [segment_tables(): centre = (2.0 * jnp.arange(8, dtype=f32) + 1.0)[None]]
    all_gather x0 -> x1, blocking collectives: none -> 97.5 us  [local(): sums = lax.all_gather(lum, ('tile', 'depth'), axis=0, tiled=True)]
    psum x1 -> x0, blocking collectives: 85.4 us -> none  [global_histogram(): return lax.psum(jnp.stack(totals), ('tile', 'depth'))]
    pallas_call x0 -> x4, Pallas kernels: none -> 78.2 us  [the longest x2 74.3 us: march(): pl.pallas_call(march_kernel, grid=(DEPTH,), in_specs=[pl.BlockSpec(memory...]
    unnamed x16 -> x18, local copies, waits for them, and re-layouts: 82.5 us -> 10.8 us
    mul x128 -> x1, other arithmetic: 62.1 us -> 0.01 us  [segment_tables(): 0.5 * (hi - lo)]
  transfers between devices with their start and end apart: 5 -> 6, of which waited for: 5 -> 2; matrix products, arithmetic and copies ran while one was open for 0% -> 4% of each run, Pallas kernels for 0% -> 15%
where the time goes in v1:
time: 241 us; the launch traced here: 240 us
  blocking collectives  97.5 us (40%)
  Pallas kernels  78.2 us (32%)
  starting transfers between devices  27.9 us (12%)
  local copies, waits for them, and re-layouts  16.9 us (7%)
  waiting for transfers between devices  14.4 us (6%)
  other arithmetic  3.42 us (1%)
    all_gather x1, blocking collectives, local(): sums = lax.all_gather(lum, ('tile', 'depth'), axis=0, tiled=True)  97.5 us
    pallas_call x2, Pallas kernels, march(): pl.pallas_call(march_kernel, grid=(DEPTH,), in_specs=[pl.BlockSpec(memory...  74.3 us
    all_to_all x2, starting transfers between devices, local(): lax.all_to_all(part, 'depth', split_axis=0, concat_axis=0, tiled=True)  15.2 us
    unnamed x18, local copies, waits for them, and re-layouts  10.8 us
    all_to_all x2, waiting for transfers between devices, local(): lax.all_to_all(part, 'depth', split_axis=0, concat_axis=0, tiled=True)  10.4 us
    ppermute x2, starting transfers between devices, neighbours(): lax.ppermute(low_source, axis, forward)  9.49 us
  transfers between devices with their start and end apart: 6, of which 2 were waited for; matrix products, arithmetic and copies ran while one was open for 4% of the time, Pallas kernels for 15%

profile of v1, /device:TPU:1, one launch (start us, length us, event | category | flops | bytes accessed | tf_op | source)
XLA Modules:
  0.0 239.9 jit_solution(7261988709069696121)
XLA Ops:
  0.0 1.0 slice_bitcast_fusion
  1.0 1.3 collective-permute-start.1
  2.3 4.6 %collective-permute-start = (bf16[16,4096]{1,0:T(8,128)(2,1)S(1)}, bf16[16,4096]{1,0:T(8,128)(2,1)S(1)}, u32[]{:S(2)}, u32[]{:S(2)}) collective-permute-start(bf16[16,4096]{1,0:T(8,128)(2,1)S(1)} %get-tuple-element.14), channel_id=1, source_target_pairs={{0,1},{1,2},{2,3},{3,4},{4,5},{5,6},{6,7},{7,8},{8,9},{9,10},{10,1... | collective-permute-start | bytes 393224 | tf_op jit(solution)/shard_map/ppermute | solution.py:204
  6.9 4.6 %fusion = (bf16[64,1,4096]{2,1,0:T(2,128)(2,1)S(1)}, bf16[64,1,4096]{2,1,0:T(2,128)(2,1)S(1)}) fusion(bf16[64,16,4096]{2,1,0:T(8,128)(2,1)} %vn_ref.3), kind=kLoop, calls=%fused_computation.12 | loop fusion | bytes 2097152 | tf_op jit(solution)/shard_map/slice | solution.py:209
  11.5 0.6 copy.22
  12.1 4.9 %collective-permute-start.2 = (bf16[64,4096]{1,0:T(8,128)(2,1)S(1)}, bf16[64,4096]{1,0:T(8,128)(2,1)S(1)}, u32[]{:S(2)}, u32[]{:S(2)}) collective-permute-start(bf16[64,4096]{1,0:T(8,128)(2,1)S(1)} %bitcast.13), channel_id=1, source_target_pairs={{0,16},{16,32},{32,48},{48,64},{64,80},{80,96},{96,112},{112,128},... | collective-permute-start | bytes 1572872 | tf_op jit(solution)/shard_map/ppermute | solution.py:204
  17.0 0.6 copy.21
  17.6 1.9 collective-permute-start.3
  19.5 0.7 pad_maximum_fusion.1
  20.2 0.1 slice.24
  20.3 0.1 slice.27
  20.4 0.1 slice.25
  20.5 1.3 multiply_reduce_fusion
  22.4 0.8 pad_maximum_fusion.2
  23.2 0.1 slice.26
  23.3 0.1 broadcast_in_dim.12
  23.4 0.7 multiply_divide_fusion.lp_ref
  24.1 0.0 collective-permute-done.1.zhi_ref
  24.1 0.0 collective-permute-done.zlo_ref
  24.1 0.0 collective-permute-done.2.ylo_ref
  24.1 4.0 %collective-permute-done.3.yhi_ref = bf16[64,4096]{1,0:T(8,128)(2,1)S(1)} collective-permute-done((bf16[64,4096]{1,0:T(8,128)(2,1)S(1)}, bf16[64,4096]{1,0:T(8,128)(2,1)S(1)}, u32[]{:S(2)}, u32[]{:S(2)}) %collective-permute-start.3) | collective-permute-done | bytes 524320 | tf_op jit(solution)/shard_map/ppermute | solution.py:204
  28.1 0.1 broadcast_in_dim.13.t_ref
  28.2 0.0 copy-start
  28.2 3.4 %copy-done = bf16[64,16,4096]{2,1,0:T(8,128)(2,1)S(1)} copy-done((bf16[64,16,4096]{2,1,0:T(8,128)(2,1)S(1)}, bf16[64,16,4096]{2,1,0:T(8,128)(2,1)}, u32[]{:S(2)}) %copy-start) | copy-done | bytes 8388632
  31.5 0.0 copy-start.2
  31.5 1.0 copy-done.2
  32.5 0.0 copy-start.4
  32.5 0.9 copy-done.4
  33.4 0.0 copy-start.3
  33.4 0.0 copy-start.5
  33.4 37.2 %march.2 = f32[16,7,16,128]{3,2,1,0:T(8,128)} custom-call(f32[3]{0:T(128)S(1)} %multiply_divide_fusion.lp_ref, f32[104,128]{1,0:T(8,128)S(1)} %broadcast_in_dim.13.t_ref, bf16[3,384,128]{2,1,0:T(8,128)(2,1)S(1)} %copy-done.2, bf16[256,384]{1,0:T(8,128)(2,1)S(1)} %copy-done.4, bf16[64,16,4096]{2,1,0:T(8,128)(2,1)S(1)} %copy-done, ...), custom_call_target="tpu_custom_call" | custom-call | flops 200000000 | bytes 12000000 | tf_op jit(solution)/shard_map/march/pallas_call | solution.py:139
  70.6 8.6 %all-to-all-start = ((f32[16,7,16,128]{3,2,1,0:T(8,128)}), f32[16,7,16,128]{3,2,1,0:T(8,128)S(1)}, u32[]{:S(2)}, u32[]{:S(2)}) async-start(f32[16,7,16,128]{3,2,1,0:T(8,128)} %march.2), calls=%async_computation | async-start | bytes 1835008 | tf_op jit(solution)/shard_map/all_to_all | solution.py:216
  79.2 0.0 copy-done.3
  79.2 0.0 copy-done.5
  79.3 0.0 copy-start.1
  79.3 3.4 %copy-done.1 = bf16[64,16,4096]{2,1,0:T(8,128)(2,1)S(1)} copy-done((bf16[64,16,4096]{2,1,0:T(8,128)(2,1)S(1)}, bf16[64,16,4096]{2,1,0:T(8,128)(2,1)}, u32[]{:S(2)}) %copy-start.1) | copy-done | bytes 8388632
  82.6 37.1 %march.3 = f32[16,7,16,128]{3,2,1,0:T(8,128)} custom-call(f32[3]{0:T(128)S(1)} %multiply_divide_fusion.lp_ref, f32[104,128]{1,0:T(8,128)S(1)} %broadcast_in_dim.13.t_ref, bf16[3,384,128]{2,1,0:T(8,128)(2,1)S(1)} %copy-done.3, bf16[256,384]{1,0:T(8,128)(2,1)S(1)} %copy-done.5, bf16[64,16,4096]{2,1,0:T(8,128)(2,1)S(1)} %copy-done.1, ...), custom_call_target="tpu_custom_call" | custom-call | flops 200000000 | bytes 12000000 | tf_op jit(solution)/shard_map/march/pallas_call | solution.py:139
  119.7 0.0 all-to-all-done.s0_ref
  119.7 0.0 copy-start.6
  119.7 6.7 %all-to-all-start.1 = ((f32[16,7,16,128]{3,2,1,0:T(8,128)}), f32[16,7,16,128]{3,2,1,0:T(8,128)S(1)}, u32[]{:S(2)}, u32[]{:S(2)}) async-start(f32[16,7,16,128]{3,2,1,0:T(8,128)} %march.3), calls=%async_computation.1 | async-start | bytes 1835008 | tf_op jit(solution)/shard_map/all_to_all | solution.py:216
  127.0 10.4 %all-to-all-done.1.s1_ref = f32[16,7,16,128]{3,2,1,0:T(8,128)S(1)} async-done(((f32[16,7,16,128]{3,2,1,0:T(8,128)}), f32[16,7,16,128]{3,2,1,0:T(8,128)S(1)}, u32[]{:S(2)}, u32[]{:S(2)}) %all-to-all-start.1) | async-done | bytes 917536 | tf_op jit(solution)/shard_map/all_to_all | solution.py:216
  137.4 0.0 copy-done.6
  137.4 0.0 copy-start.7
  137.4 1.0 copy-done.7
  138.4 2.2 composite.1
  140.6 97.5 %all-gather = f32[256,1,128]{2,1,0:T(1,128)} all-gather(f32[1,1,128]{2,1,0:T(1,128)} %bitcast.18), channel_id=1, replica_groups=mesh['tile'=16,'depth'=16] {'tile','depth'}, dimensions={0}, use_global_device_ids=true | all-gather | bytes 131584 | tf_op jit(solution)/shard_map/all_gather | solution.py:230
  238.1 1.8 finish.1
  (3 shorter events, 0.0 us)
Async XLA Ops:
  1.0 23.1 %collective-permute-start.1 = (bf16[16,4096]{1,0:T(8,128)(2,1)S(1)}, bf16[16,4096]{1,0:T(8,128)(2,1)S(1)}, u32[]{:S(2)}, u32[]{:S(2)}) collective-permute-start(bf16[16,4096]{1,0:T(8,128)(2,1)S(1)} %get-tuple-element.13), channel_id=1, source_target_pairs={{1,0},{2,1},{3,2},{4,3},{5,4},{6,5},{7,6},{8,7},{9,8},{10,9},{11,1... | collective-permute-start | bytes 393224 | tf_op jit(solution)/shard_map/ppermute | solution.py:204
  2.3 21.8 %collective-permute-start = (bf16[16,4096]{1,0:T(8,128)(2,1)S(1)}, bf16[16,4096]{1,0:T(8,128)(2,1)S(1)}, u32[]{:S(2)}, u32[]{:S(2)}) collective-permute-start(bf16[16,4096]{1,0:T(8,128)(2,1)S(1)} %get-tuple-element.14), channel_id=1, source_target_pairs={{0,1},{1,2},{2,3},{3,4},{4,5},{5,6},{6,7},{7,8},{8,9},{9,10},{10,1... | collective-permute-start | bytes 393224 | tf_op jit(solution)/shard_map/ppermute | solution.py:204
  12.1 12.0 %collective-permute-start.2 = (bf16[64,4096]{1,0:T(8,128)(2,1)S(1)}, bf16[64,4096]{1,0:T(8,128)(2,1)S(1)}, u32[]{:S(2)}, u32[]{:S(2)}) collective-permute-start(bf16[64,4096]{1,0:T(8,128)(2,1)S(1)} %bitcast.13), channel_id=1, source_target_pairs={{0,16},{16,32},{32,48},{48,64},{64,80},{80,96},{96,112},{112,128},... | collective-permute-start | bytes 1572872 | tf_op jit(solution)/shard_map/ppermute | solution.py:204
  17.6 10.5 %collective-permute-start.3 = (bf16[64,4096]{1,0:T(8,128)(2,1)S(1)}, bf16[64,4096]{1,0:T(8,128)(2,1)S(1)}, u32[]{:S(2)}, u32[]{:S(2)}) collective-permute-start(bf16[64,4096]{1,0:T(8,128)(2,1)S(1)} %bitcast.14), channel_id=1, source_target_pairs={{16,0},{32,16},{48,32},{64,48},{80,64},{96,80},{112,96},{128,112},... | collective-permute-start | bytes 1572872 | tf_op jit(solution)/shard_map/ppermute | solution.py:204
  28.2 3.4 %copy-start = (bf16[64,16,4096]{2,1,0:T(8,128)(2,1)S(1)}, bf16[64,16,4096]{2,1,0:T(8,128)(2,1)}, u32[]{:S(2)}) copy-start(bf16[64,16,4096]{2,1,0:T(8,128)(2,1)} %vn_ref.3) | copy-start | bytes 25165828
  31.5 1.0 copy-start.2
  32.5 0.9 copy-start.4
  33.4 45.8 %copy-start.3 = (bf16[3,384,128]{2,1,0:T(8,128)(2,1)S(1)}, bf16[3,384,128]{2,1,0:T(8,128)(2,1)}, u32[]{:S(2)}) copy-start(bf16[3,384,128]{2,1,0:T(8,128)(2,1)} %constant.6.clone.sx_ref) | copy-start | bytes 884740
  33.4 45.8 %copy-start.5 = (bf16[256,384]{1,0:T(8,128)(2,1)S(1)}, bf16[256,384]{1,0:T(8,128)(2,1)}, u32[]{:S(2)}) copy-start(bf16[256,384]{1,0:T(8,128)(2,1)} %constant.16.clone.sy_ref) | copy-start | bytes 589828
  70.6 49.1 %all-to-all-start = ((f32[16,7,16,128]{3,2,1,0:T(8,128)}), f32[16,7,16,128]{3,2,1,0:T(8,128)S(1)}, u32[]{:S(2)}, u32[]{:S(2)}) async-start(f32[16,7,16,128]{3,2,1,0:T(8,128)} %march.2), calls=%async_computation | async-start | bytes 1835008 | tf_op jit(solution)/shard_map/all_to_all | solution.py:216
  79.3 3.4 %copy-start.1 = (bf16[64,16,4096]{2,1,0:T(8,128)(2,1)S(1)}, bf16[64,16,4096]{2,1,0:T(8,128)(2,1)}, u32[]{:S(2)}) copy-start(bf16[64,16,4096]{2,1,0:T(8,128)(2,1)} %vn_ref.3) | copy-start | bytes 25165828
  119.7 17.7 %copy-start.6 = (f32[16,7,16,128]{3,2,1,0:T(8,128)}, f32[16,7,16,128]{3,2,1,0:T(8,128)S(1)}, u32[]{:S(2)}) copy-start(f32[16,7,16,128]{3,2,1,0:T(8,128)S(1)} %all-to-all-done.s0_ref) | copy-start | bytes 2752516
  119.7 17.7 %all-to-all-start.1 = ((f32[16,7,16,128]{3,2,1,0:T(8,128)}), f32[16,7,16,128]{3,2,1,0:T(8,128)S(1)}, u32[]{:S(2)}, u32[]{:S(2)}) async-start(f32[16,7,16,128]{3,2,1,0:T(8,128)} %march.3), calls=%async_computation.1 | async-start | bytes 1835008 | tf_op jit(solution)/shard_map/all_to_all | solution.py:216
  137.4 1.0 copy-start.7

commit v2 on v1

v2 whole, which is shorter than its diff:
```python
import functools
import math

import jax
import jax.numpy as jnp
import numpy as np
from jax import lax
from jax.experimental import pallas as pl
from jax.experimental.pallas import tpu as pltpu
from jax.sharding import PartitionSpec as P

f32 = jnp.float32
bf16 = jnp.bfloat16

BINS = 64
AMBIENT = 0.3
LUMA_EPS = 0.01
LOG_LOW = math.log(0.01)
LOG_HIGH = 0.05
EXPOSURE_KEY = 0.25
BIN_WIDTH = (LOG_HIGH - LOG_LOW) / (BINS - 1)

PLANES = 64
ROWS = 16
LANES = 128
DEPTH = 16
WIDE = 256
KNOTS = 16
VMEM = 58 * 1024 * 1024


def difference_matrices():
    base = np.zeros((512, WIDE), np.float32)
    for i in range(WIDE):
        base[LANES + i - 1, i] = -1
        base[LANES + i + 1, i] = 1
    first = base.copy()
    first[:LANES] = 0
    last = base.copy()
    last[LANES + WIDE :] = 0
    sy = np.zeros((2, 128, WIDE), np.float32)
    for e in range(2):
        for p in range(8):
            for r in range(ROWS):
                o = ROWS * p + r
                sy[e, o, o - 1 if r > 0 else 128 + 8 * e + p] = -1
                sy[e, o, o + 1 if r < ROWS - 1 else 144 + 8 * e + p] = 1
    return jnp.asarray(np.stack([first, base, last]), bf16), jnp.asarray(sy, bf16)


def pick(table, index):
    return jnp.take_along_axis(table, index, axis=0, mode="promise_in_bounds")


def halves(x):
    x = x.astype(f32)
    return [x[0:8], x[8:16]]


def march_kernel(
    light_ref, color_ref, opacity_ref, sxf_ref, sx_ref, sxl_ref, sy_ref,
    before_ref, cur_ref, next_ref, after_ref,
    zlo_ref, zhi_ref, ylo_ref, yhi_ref, ylon_ref, yhin_ref,
    front_ref, back_ref, dxa, dya, dxb, dyb, acc, table,
):
    s = pl.program_id(0)
    squares = light_ref[0] * light_ref[0] + light_ref[1] * light_ref[1] + light_ref[2] * light_ref[2]
    scale = (0.5 * (1.0 - AMBIENT)) * lax.rsqrt(jnp.full((8, LANES), squares + 1.0, f32))
    lz, ly, lx = light_ref[0] * scale, light_ref[1] * scale, light_ref[2] * scale

    def differences(g, part, pieces, matrix, before, after, block, dx, dy):
        ref, cols = block
        planes = pl.ds(pl.multiple_of(16 * g, 16), 16)
        if part == 0:
            wide = jnp.concatenate(
                [r[planes, :, c].reshape(256, c.stop - c.start) for r, c in pieces], axis=1
            )
            rows = pl.ds(pl.multiple_of(256 * g, 256), 256)
            dx[rows, :] = jnp.dot(wide, matrix[...], preferred_element_type=f32)
        else:
            edges = [r[planes, c] for r, c in (before, after)]
            fill = jnp.zeros((96, WIDE), bf16)
            for e in range(2):
                some = pl.ds(pl.multiple_of(16 * g + 8 * e, 8), 8)
                rows = pl.ds(pl.multiple_of(256 * g + 128 * e, 128), 128)
                tall = jnp.concatenate([ref[some, :, cols].reshape(128, WIDE), *edges, fill], axis=0)
                dy[rows, :] = jnp.dot(sy_ref[e], tall, preferred_element_type=f32)

    low, high = slice(0, WIDE), slice(WIDE, 2 * WIDE)
    first = (
        [(before_ref, slice(0, 128)), (cur_ref, slice(0, 384))],
        sxf_ref, (ylo_ref, low), (yhi_ref, low), (cur_ref, low), dxa, dya,
    )
    odd = (
        [(cur_ref, slice(128, 512)), (next_ref, slice(0, 128))],
        sxl_ref, (ylo_ref, high), (yhi_ref, high), (cur_ref, high), dxb, dyb,
    )
    even = (
        [(cur_ref, slice(384, 512)), (next_ref, low), (after_ref, slice(0, 128))],
        sx_ref, (ylon_ref, low), (yhin_ref, low), (next_ref, low), dxa, dya,
    )

    @pl.when(s == 0)
    def _():
        for k in range(4):
            f = [color_ref[k - 1, i] if k else opacity_ref[i] for i in range(KNOTS)]
            for j in range(8):
                mid = f[2 * j + 1]
                rise = f[2 * j + 2] - mid if j < 7 else 0.0
                for row, value in ((k, mid), (4 + k, mid - f[2 * j]), (8 + k, rise)):
                    table[8 * row + j : 8 * row + j + 1, :] = jnp.full((1, LANES), value, f32)
        for j in range(8):
            table[96 + j : 97 + j, :] = jnp.full((1, LANES), 2.0 * j + 1.0, f32)
        for g in range(4):
            for part in range(2):
                differences(g, part, *first)

    tb = [table[8 * k : 8 * k + 8, :] for k in range(13)]

    def sample(below, v, above, dx, dy, state):
        dz = above - below
        q = (dz * dz + 0.16) + (dy * dy + dx * dx)
        dot = (dz * lz + dy * ly) + dx * lx
        shade = (AMBIENT + 0.5 * (1.0 - AMBIENT)) + dot * lax.rsqrt(q)
        j = (v * 7.5).astype(jnp.int32)
        u = v * 15.0 - pick(tb[12], j)
        left = u < 0.0
        alpha, red, green, blue = [
            pick(tb[k], j) + jnp.where(left, pick(tb[4 + k], j), pick(tb[8 + k], j)) * u
            for k in range(4)
        ]
        w = alpha * shade
        keep = 1.0 - alpha
        p = [w * c for c in (red, green, blue)]
        through = state[3]
        return (
            [state[i] + through * p[i] for i in range(3)]
            + [through * keep]
            + [state[4 + i] * keep + p[i] for i in range(3)]
        )

    for half, (dx, dy, following) in enumerate(((dxa, dya, odd), (dxb, dyb, even))):
        for side in range(2):
            for h in range(2):
                for i in range(7):
                    acc[side, h, i] = jnp.full((8, LANES), 1.0 if i == 3 else 0.0, f32)

        def group(g, unused, half=half, dx=dx, dy=dy, following=following):
            for side in range(2):
                differences(g, side, *following)
                lanes = slice(LANES * side, LANES * side + LANES)
                at = WIDE * half + LANES * side
                cols = slice(at, at + LANES)
                lo = jnp.where(g == 0, zlo_ref[:, cols], cur_ref[jnp.maximum(16 * g - 1, 0), :, cols])
                hi = jnp.where(
                    g == 3, zhi_ref[:, cols], cur_ref[jnp.minimum(16 * g + 16, PLANES - 1), :, cols]
                )
                below, here = halves(lo), halves(cur_ref[16 * g, :, cols])
                state = [[acc[side, h, i] for i in range(7)] for h in range(2)]
                for p in range(16):
                    above = halves(cur_ref[16 * g + p + 1, :, cols] if p < 15 else hi)
                    for h in range(2):
                        rows = pl.ds(pl.multiple_of(256 * g + 16 * p + 8 * h, 8), 8)
                        state[h] = sample(
                            below[h], here[h], above[h], dx[rows, lanes], dy[rows, lanes], state[h]
                        )
                    below, here = here, above
                for h in range(2):
                    for i in range(7):
                        acc[side, h, i] = state[h][i]
            return unused

        lax.fori_loop(0, 4, group, 0, unroll=4)
        for side in range(2):
            lanes = slice(LANES * side, LANES * side + LANES)
            for h in range(2):
                rows = slice(8 * h, 8 * h + 8)
                for i in range(3):
                    front_ref[half, i, rows, lanes] = acc[side, h, i]
                    back_ref[half, i, rows, lanes] = acc[side, h, 4 + i]
                front_ref[half, 3, rows, lanes] = 1.0 - acc[side, h, 3]


def march(vol, zlo, zhi, ylo, yhi, light, tf_color, tf_opacity):
    sx, sy = difference_matrices()
    steps = DEPTH // 2

    def follower(s):
        return jnp.minimum(2 * s + 2, DEPTH - 1)

    def block(width, place):
        return pl.BlockSpec((PLANES, ROWS, width), lambda s: (0, 0, place(s)))

    def matrix(place):
        return pl.BlockSpec((None, 512, WIDE), lambda s: (place(s), 0, 0))

    def edge(rows, width, place):
        return pl.BlockSpec((rows, width), lambda s: (0, place(s)))

    smem = pl.BlockSpec(memory_space=pltpu.SMEM)
    return pl.pallas_call(
        march_kernel,
        grid=(steps,),
        in_specs=[
            smem,
            smem,
            smem,
            matrix(lambda s: 0),
            matrix(lambda s: 1),
            matrix(lambda s: jnp.where(s == steps - 1, 2, 1)),
            pl.BlockSpec((2, 128, WIDE), lambda s: (0, 0, 0)),
            block(LANES, lambda s: 0),
            block(2 * WIDE, lambda s: s),
            block(WIDE, follower),
            block(LANES, lambda s: jnp.minimum(4 * s + 6, 2 * DEPTH - 1)),
            edge(ROWS, 2 * WIDE, lambda s: s),
            edge(ROWS, 2 * WIDE, lambda s: s),
            edge(PLANES, 2 * WIDE, lambda s: s),
            edge(PLANES, 2 * WIDE, lambda s: s),
            edge(PLANES, WIDE, follower),
            edge(PLANES, WIDE, follower),
        ],
        out_specs=[
            pl.BlockSpec((2, n, ROWS, WIDE), lambda s: (s, 0, 0, 0)) for n in (4, 3)
        ],
        out_shape=[jax.ShapeDtypeStruct((DEPTH, n, ROWS, WIDE), f32) for n in (4, 3)],
        scratch_shapes=[pltpu.VMEM((PLANES * ROWS, WIDE), f32)] * 4
        + [pltpu.VMEM((2, 2, 7, 8, LANES), f32), pltpu.VMEM((104, LANES), f32)],
        compiler_params=pltpu.CompilerParams(vmem_limit_bytes=VMEM),
        cost_estimate=pl.CostEstimate(
            flops=400_000_000, bytes_accessed=24_000_000, transcendentals=4_000_000
        ),
        name="march",
    )(
        light, tf_color, tf_opacity, sx, sx, sx, sy, vol, vol, vol, vol,
        zlo, zhi, ylo, yhi, ylo, yhi,
    )


def front_kernel(bg_ref, prior_ref, s_ref, mapped_ref, lum_ref):
    total = jnp.zeros((8, LANES), f32)
    for c in range(2):
        cols = slice(LANES * c, LANES * c + LANES)
        front = [s_ref[0, i, :, cols] for i in range(3)]
        through = 1.0 - s_ref[0, 3, :, cols]
        for d in range(1, DEPTH):
            front = [front[i] + through * s_ref[d, i, :, cols] for i in range(3)]
            through = through - through * s_ref[d, 3, :, cols]
        front = [front[i] + through * bg_ref[i] for i in range(3)]
        lum = jnp.log(0.2126 * front[0] + 0.7152 * front[1] + 0.0722 * front[2] + LUMA_EPS)
        near = jnp.clip(lum, LOG_LOW, LOG_HIGH)
        term = near * jnp.maximum(0.0, 1.0 - jnp.abs(lum - near) * (1.0 / BIN_WIDTH))
        total = total + term[0:8] + term[8:16]
        for i in range(3):
            scaled = prior_ref[0] * front[i]
            mapped_ref[i, :, cols] = scaled / (1.0 + scaled)
    lum_ref[...] = total


def back_kernel(bg_ref, f_ref, s_ref, second_ref):
    for c in range(2):
        cols = slice(LANES * c, LANES * c + LANES)
        back = [s_ref[0, i, :, cols] for i in range(3)]
        through = 1.0 - f_ref[0, 3, :, cols]
        for d in range(1, DEPTH):
            keep = 1.0 - f_ref[d, 3, :, cols]
            back = [s_ref[d, i, :, cols] + keep * back[i] for i in range(3)]
            through = through * keep
        for i in range(3):
            second_ref[i, :, cols] = back[i] + through * bg_ref[i]


def finish_kernel(pixels, lum_ref, mapped_ref, second_ref, o_ref):
    total = jnp.sum(jnp.sum(lum_ref[...], axis=0), axis=(0, 1), keepdims=True)
    exposure = EXPOSURE_KEY * jnp.exp(-total / pixels)
    for i in range(3):
        o_ref[0, i] = mapped_ref[i]
        scaled = exposure * second_ref[i]
        o_ref[1, i] = scaled / (1.0 + scaled)


def neighbours(low_source, high_source, axis):
    count = lax.axis_size(axis)
    forward = [(i, i + 1) for i in range(count - 1)]
    backward = [(target, source) for source, target in forward]
    return lax.ppermute(low_source, axis, forward), lax.ppermute(high_source, axis, backward)


def to_columns(part):
    part = lax.all_to_all(part.astype(jnp.float16), "depth", split_axis=0, concat_axis=0, tiled=True)
    return part.astype(f32)


def local(volume, tf_color, tf_opacity, light, background, exposure_prior):
    ylo, yhi = neighbours(volume[:, ROWS - 1], volume[:, 0], "tile")
    zlo, zhi = neighbours(volume[PLANES - 1], volume[0], "depth")
    front, back = march(volume, zlo, zhi, ylo, yhi, light, tf_color, tf_opacity)
    smem = pl.BlockSpec(memory_space=pltpu.SMEM)
    vmem = pl.BlockSpec(memory_space=pltpu.VMEM)
    image = jax.ShapeDtypeStruct((3, ROWS, WIDE), f32)
    front = to_columns(front)
    mapped, lum = pl.pallas_call(
        front_kernel,
        in_specs=[smem, smem, vmem],
        out_specs=[vmem] * 2,
        out_shape=[image, jax.ShapeDtypeStruct((8, LANES), f32)],
        name="front",
    )(background, exposure_prior, front)
    lum, back = lax.optimization_barrier((lum, back))
    sums = lax.all_gather(lum, ("tile", "depth"), axis=0, tiled=False)
    back = to_columns(back)
    second = pl.pallas_call(
        back_kernel, in_specs=[smem, vmem, vmem], out_specs=vmem, out_shape=image, name="back"
    )(background, front, back)
    pixels = ROWS * lax.axis_size("tile") * volume.shape[2]
    return pl.pallas_call(
        functools.partial(finish_kernel, float(pixels)),
        in_specs=[vmem] * 3,
        out_specs=vmem,
        out_shape=jax.ShapeDtypeStruct((2, 3, ROWS, WIDE), f32),
        name="finish",
    )(sums, mapped, second)


def solution(mesh):
    placed = (P("depth", "tile", None), P(), P(), P(), P(), P())
    return jax.shard_map(
        local, mesh=mesh, in_specs=placed, out_specs=P(None, None, "tile", "depth"), check_vma=False
    )
```

time: 241 us -> 212 us (0.88)
  waiting for transfers between devices: 14.4 us -> 102 us
  blocking collectives: 97.5 us -> 11.9 us
  Pallas kernels: 78.2 us -> 50.5 us
  between operations: 1.48 us -> 14.1 us
  local copies, waits for them, and re-layouts: 16.9 us -> 8.43 us
  starting transfers between devices: 27.9 us -> 19.6 us
    all_gather x1 -> x0, blocking collectives: 97.5 us -> none  [local(): sums = lax.all_gather(lum, ('tile', 'depth'), axis=0, tiled=True)]
    all_gather x0 -> x1, waiting for transfers between devices: none -> 85.9 us  [local(): sums = lax.all_gather(lum, ('tile', 'depth'), axis=0, tiled=False)]
    pallas_call x3, Pallas kernels: 76.5 us -> 48.2 us  [the longest x1 44.1 us: march(): pl.pallas_call(march_kernel, grid=(steps,), in_specs=[smem, smem, smem, m...]
    all_to_all x0 -> x1, blocking collectives: none -> 11.9 us  [to_columns(): lax.all_to_all(part.astype(jnp.float16), 'depth', split_axis=0, concat_ax...]
    unnamed x18 -> x10, local copies, waits for them, and re-layouts: 10.8 us -> 2.84 us
    all_to_all x2 -> x1, starting transfers between devices: 15.2 us -> 8.3 us  [to_columns(): lax.all_to_all(part.astype(jnp.float16), 'depth', split_axis=0, concat_ax...]
    convert_element_type x0 -> x4, other arithmetic: none -> 5.5 us  [the longest x2 3.38 us: to_columns(): part.astype(jnp.float16)]
    all_to_all x2 -> x1, waiting for transfers between devices: 10.4 us -> 11.4 us  [to_columns(): lax.all_to_all(part.astype(jnp.float16), 'depth', split_axis=0, concat_ax...]
  transfers between devices with their start and end apart: 6 -> 6, of which waited for: 2 -> 4; matrix products, arithmetic and copies ran while one was open for 4% -> 2% of each run, Pallas kernels for 15% -> 1%
where the time goes in v2:
time: 212 us
  waiting for transfers between devices  102 us (48%)
  Pallas kernels  50.5 us (24%)
  starting transfers between devices  19.6 us (9%)
  between operations  14.1 us (7%)
  blocking collectives  11.9 us (6%)
  local copies, waits for them, and re-layouts  8.43 us (4%)
  other arithmetic  5.5 us (3%)
    all_gather x1, waiting for transfers between devices, local(): sums = lax.all_gather(lum, ('tile', 'depth'), axis=0, tiled=False)  85.9 us
    pallas_call x1, Pallas kernels, march(): pl.pallas_call(march_kernel, grid=(steps,), in_specs=[smem, smem, smem, m...  44.1 us
    all_to_all x1, blocking collectives, to_columns(): lax.all_to_all(part.astype(jnp.float16), 'depth', split_axis=0, concat_ax...  11.9 us
    all_to_all x1, waiting for transfers between devices, to_columns(): lax.all_to_all(part.astype(jnp.float16), 'depth', split_axis=0, concat_ax...  11.4 us
    all_to_all x1, starting transfers between devices, to_columns(): lax.all_to_all(part.astype(jnp.float16), 'depth', split_axis=0, concat_ax...  8.3 us
    ppermute x2, starting transfers between devices, neighbours(): lax.ppermute(low_source, axis, forward)  8.06 us
    slice x1, local copies, waits for them, and re-layouts, local(): ylo, yhi = neighbours(volume[:, ROWS - 1], volume[:, 0], 'tile')  4.6 us
  transfers between devices with their start and end apart: 6, of which 4 were waited for; matrix products, arithmetic and copies ran while one was open for 2% of the time, Pallas kernels for 1%

profile of v2, /device:TPU:1, one launch (start us, length us, event | category | flops | bytes accessed | tf_op | source)
XLA Modules:
  0.0 211.9 jit_solution(10823299864160956464)
XLA Ops:
  6.5 4.6 %fusion = (bf16[64,1,4096]{2,1,0:T(2,128)(2,1)S(1)}, bf16[64,1,4096]{2,1,0:T(2,128)(2,1)S(1)}) fusion(bf16[64,16,4096]{2,1,0:T(8,128)(2,1)} %after_ref.1), kind=kLoop, calls=%fused_computation.4 | loop fusion | bytes 2097152 | tf_op jit(solution)/shard_map/slice | solution.py:295
  11.1 0.6 copy.16
  11.7 4.9 %collective-permute-start.2 = (bf16[64,4096]{1,0:T(8,128)(2,1)S(1)}, bf16[64,4096]{1,0:T(8,128)(2,1)S(1)}, u32[]{:S(2)}, u32[]{:S(2)}) collective-permute-start(bf16[64,4096]{1,0:T(8,128)(2,1)S(1)} %bitcast.12), channel_id=1, source_target_pairs={{0,16},{16,32},{32,48},{48,64},{64,80},{80,96},{96,112},{112,128},... | collective-permute-start | bytes 1572872 | tf_op jit(solution)/shard_map/ppermute | solution.py:286
  16.7 0.6 copy.15
  17.3 1.9 collective-permute-start.3
  19.2 1.0 slice_bitcast_fusion
  20.2 3.1 %collective-permute-start = (bf16[16,4096]{1,0:T(8,128)(2,1)S(1)}, bf16[16,4096]{1,0:T(8,128)(2,1)S(1)}, u32[]{:S(2)}, u32[]{:S(2)}) collective-permute-start(bf16[16,4096]{1,0:T(8,128)(2,1)S(1)} %get-tuple-element.20), channel_id=1, source_target_pairs={{0,1},{1,2},{2,3},{3,4},{4,5},{5,6},{6,7},{7,8},{8,9},{9,10},{10,1... | collective-permute-start | bytes 393224 | tf_op jit(solution)/shard_map/ppermute | solution.py:286
  23.3 1.3 collective-permute-start.1
  24.6 0.6 collective-permute-done.zlo_ref
  25.2 0.0 copy-start.2
  25.2 3.8 %collective-permute-done.1.zhi_ref = bf16[16,4096]{1,0:T(8,128)(2,1)S(1)} collective-permute-done((bf16[16,4096]{1,0:T(8,128)(2,1)S(1)}, bf16[16,4096]{1,0:T(8,128)(2,1)S(1)}, u32[]{:S(2)}, u32[]{:S(2)}) %collective-permute-start.1) | collective-permute-done | bytes 131104 | tf_op jit(solution)/shard_map/ppermute | solution.py:286
  29.0 0.0 copy-start.3
  29.0 0.0 collective-permute-done.2.ylo_ref.ylon_ref
  29.0 0.0 copy-start
  29.0 0.0 collective-permute-done.3.yhi_ref.yhin_ref
  29.0 0.0 copy-done.2
  29.0 0.6 copy-done.3
  29.7 0.2 copy-done
  29.9 0.0 copy-start.1
  29.9 0.8 copy-done.1
  30.7 44.1 %march.1 = (f32[16,4,16,256]{3,2,1,0:T(8,128)}, f32[16,3,16,256]{3,2,1,0:T(8,128)}) custom-call(f32[3]{0:T(128)} %light_ref.1, f32[3,16]{1,0:T(4,128)} %color_ref.1, f32[16]{0:T(128)} %opacity_ref.1, bf16[3,512,256]{2,1,0:T(8,128)(2,1)} %constant.4.clone.sxf_ref.sx_ref.sxl_ref, bf16[3,512,256]{2,1,0:T(8,128)(2,1)} %constant.4.clone.sxf_ref.sx_ref.sxl_ref, ...), custom_call_target="tpu_custom_call" | custom-call | flops 400000000 | bytes 24000000 | tf_op jit(solution)/shard_map/march/pallas_call | solution.py:201
  74.9 2.2 %convert_element_type.12 = f16[16,4,16,256]{3,2,1,0:T(8,128)(2,1)} convert(f32[16,4,16,256]{3,2,1,0:T(8,128)} %get-tuple-element.11) | non-fusion elementwise | flops 262144 | bytes 1572864 | tf_op jit(solution)/shard_map/convert_element_type | solution.py:290
  77.0 8.3 %all-to-all-start = ((f16[16,4,16,256]{3,2,1,0:T(8,128)(2,1)}), f16[16,4,16,256]{3,2,1,0:T(8,128)(2,1)S(1)}, u32[]{:S(2)}, u32[]{:S(2)}) async-start(f16[16,4,16,256]{3,2,1,0:T(8,128)(2,1)} %convert_element_type.12), calls=%async_computation | async-start | bytes 1048576 | tf_op jit(solution)/shard_map/all_to_all | solution.py:290
  85.4 0.0 all-gather.3.cloned.1.call-start
  86.0 11.4 %all-to-all-done = f16[16,4,16,256]{3,2,1,0:T(8,128)(2,1)S(1)} async-done(((f16[16,4,16,256]{3,2,1,0:T(8,128)(2,1)}), f16[16,4,16,256]{3,2,1,0:T(8,128)(2,1)S(1)}, u32[]{:S(2)}, u32[]{:S(2)}) %all-to-all-start) | async-done | bytes 524320 | tf_op jit(solution)/shard_map/all_to_all | solution.py:290
  97.5 1.1 convert_element_type.13.s_ref.f_ref
  98.6 2.0 front.1
  100.6 0.0 all-gather.3.cloned.1.call-update
  100.6 1.2 convert_element_type.14
  101.8 11.9 %all_to_all.10 = f16[16,3,16,256]{3,2,1,0:T(8,128)(2,1)S(1)} all-to-all(f16[16,3,16,256]{3,2,1,0:T(8,128)(2,1)S(1)} %convert_element_type.14), channel_id=1, replica_groups=mesh['tile'=16,'depth'=16] {'depth'}, dimensions={0} | all-to-all | bytes 786432 | tf_op jit(solution)/shard_map/all_to_all | solution.py:290
  113.7 1.0 convert_element_type.15.s_ref
  114.7 2.1 %back.1.second_ref = f32[3,16,256]{2,1,0:T(8,128)} custom-call(f32[3]{0:T(128)} %bg_ref.3, f32[16,4,16,256]{3,2,1,0:T(8,128)} %convert_element_type.13.s_ref.f_ref, f32[16,3,16,256]{3,2,1,0:T(8,128)} %convert_element_type.15.s_ref), custom_call_target="tpu_custom_call" | custom-call | tf_op jit(solution)/shard_map/back/pallas_call | solution.py:312
  116.9 85.9 %all-gather.3.cloned.1.call-done = f32[2048,128]{1,0:T(8,128)} async-done(((f32[8,128]{1,0:T(8,128)}), f32[2048,128]{1,0:T(8,128)}) %all-gather.3.cloned.1.call-update) | async-done | bytes 1048592 | tf_op jit(solution)/shard_map/all_gather | solution.py:310
  202.8 2.3 %finish.1 = f32[2,3,16,256]{3,2,1,0:T(8,128)} custom-call(f32[256,8,128]{2,1,0:T(8,128)} %bitcast.11, f32[3,16,256]{2,1,0:T(8,128)} %get-tuple-element.15.mapped_ref, f32[3,16,256]{2,1,0:T(8,128)} %back.1.second_ref), custom_call_target="tpu_custom_call" | custom-call | tf_op jit(solution)/shard_map/finish/pallas_call | solution.py:316
Async XLA Ops:
  11.7 17.3 %collective-permute-start.2 = (bf16[64,4096]{1,0:T(8,128)(2,1)S(1)}, bf16[64,4096]{1,0:T(8,128)(2,1)S(1)}, u32[]{:S(2)}, u32[]{:S(2)}) collective-permute-start(bf16[64,4096]{1,0:T(8,128)(2,1)S(1)} %bitcast.12), channel_id=1, source_target_pairs={{0,16},{16,32},{32,48},{48,64},{64,80},{80,96},{96,112},{112,128},... | collective-permute-start | bytes 1572872 | tf_op jit(solution)/shard_map/ppermute | solution.py:286
  17.3 11.8 %collective-permute-start.3 = (bf16[64,4096]{1,0:T(8,128)(2,1)S(1)}, bf16[64,4096]{1,0:T(8,128)(2,1)S(1)}, u32[]{:S(2)}, u32[]{:S(2)}) collective-permute-start(bf16[64,4096]{1,0:T(8,128)(2,1)S(1)} %bitcast.13), channel_id=1, source_target_pairs={{16,0},{32,16},{48,32},{64,48},{80,64},{96,80},{112,96},{128,112},... | collective-permute-start | bytes 1572872 | tf_op jit(solution)/shard_map/ppermute | solution.py:286
  20.2 5.1 %collective-permute-start = (bf16[16,4096]{1,0:T(8,128)(2,1)S(1)}, bf16[16,4096]{1,0:T(8,128)(2,1)S(1)}, u32[]{:S(2)}, u32[]{:S(2)}) collective-permute-start(bf16[16,4096]{1,0:T(8,128)(2,1)S(1)} %get-tuple-element.20), channel_id=1, source_target_pairs={{0,1},{1,2},{2,3},{3,4},{4,5},{5,6},{6,7},{7,8},{8,9},{9,10},{10,1... | collective-permute-start | bytes 393224 | tf_op jit(solution)/shard_map/ppermute | solution.py:286
  23.3 5.7 %collective-permute-start.1 = (bf16[16,4096]{1,0:T(8,128)(2,1)S(1)}, bf16[16,4096]{1,0:T(8,128)(2,1)S(1)}, u32[]{:S(2)}, u32[]{:S(2)}) collective-permute-start(bf16[16,4096]{1,0:T(8,128)(2,1)S(1)} %get-tuple-element.19), channel_id=1, source_target_pairs={{1,0},{2,1},{3,2},{4,3},{5,4},{6,5},{7,6},{8,7},{9,8},{10,9},{11,1... | collective-permute-start | bytes 393224 | tf_op jit(solution)/shard_map/ppermute | solution.py:286
  25.2 3.8 %copy-start.2 = (bf16[16,4096]{1,0:T(8,128)(2,1)}, bf16[16,4096]{1,0:T(8,128)(2,1)S(1)}, u32[]{:S(2)}) copy-start(bf16[16,4096]{1,0:T(8,128)(2,1)S(1)} %collective-permute-done.zlo_ref) | copy-start | bytes 393220
  29.0 0.6 copy-start.3
  29.0 0.9 copy-start
  29.9 0.8 copy-start.1
  77.0 20.4 %all-to-all-start = ((f16[16,4,16,256]{3,2,1,0:T(8,128)(2,1)}), f16[16,4,16,256]{3,2,1,0:T(8,128)(2,1)S(1)}, u32[]{:S(2)}, u32[]{:S(2)}) async-start(f16[16,4,16,256]{3,2,1,0:T(8,128)(2,1)} %convert_element_type.12), calls=%async_computation | async-start | bytes 1048576 | tf_op jit(solution)/shard_map/all_to_all | solution.py:290
  85.4 117.4 %all-gather.3.cloned.1.call-start = ((), (), s32[]{:S(2)}) async-start(), calls=%async_computation.2 | async-start | bytes 1052672 | tf_op jit(solution)/shard_map/all_gather | solution.py:310
Sparse Core Ops, SparseCore 0:
  100.7 102.0 all-gather.2

commit v3 on v2

--- a/solution.py
+++ b/solution.py
@@ -11,6 +11,7 @@
 
 f32 = jnp.float32
 bf16 = jnp.bfloat16
+f16 = jnp.float16
 
 BINS = 64
 AMBIENT = 0.3
@@ -254,7 +255,8 @@
         for i in range(3):
             scaled = prior_ref[0] * front[i]
             mapped_ref[i, :, cols] = scaled / (1.0 + scaled)
-    lum_ref[...] = total
+    coarse = jnp.round(total * 64.0) * (1.0 / 64.0)
+    lum_ref[...] = jnp.concatenate([coarse, total - coarse], axis=1)
 
 
 def back_kernel(bg_ref, f_ref, s_ref, second_ref):
@@ -286,9 +288,8 @@
     return lax.ppermute(low_source, axis, forward), lax.ppermute(high_source, axis, backward)
 
 
-def to_columns(part):
-    part = lax.all_to_all(part.astype(jnp.float16), "depth", split_axis=0, concat_axis=0, tiled=True)
-    return part.astype(f32)
+def exchange(part, axis):
+    return lax.all_to_all(part, axis, split_axis=0, concat_axis=0, tiled=True)
 
 
 def local(volume, tf_color, tf_opacity, light, background, exposure_prior):
@@ -298,20 +299,22 @@
     smem = pl.BlockSpec(memory_space=pltpu.SMEM)
     vmem = pl.BlockSpec(memory_space=pltpu.VMEM)
     image = jax.ShapeDtypeStruct((3, ROWS, WIDE), f32)
-    front = to_columns(front)
+    front = exchange(front.astype(f16), "depth").astype(f32)
     mapped, lum = pl.pallas_call(
         front_kernel,
         in_specs=[smem, smem, vmem],
         out_specs=[vmem] * 2,
-        out_shape=[image, jax.ShapeDtypeStruct((8, LANES), f32)],
+        out_shape=[image, jax.ShapeDtypeStruct((8, WIDE), f32)],
         name="front",
     )(background, exposure_prior, front)
-    lum, back = lax.optimization_barrier((lum, back))
-    sums = lax.all_gather(lum, ("tile", "depth"), axis=0, tiled=False)
-    back = to_columns(back)
+    lum = jnp.broadcast_to(jnp.pad(lum, ((0, 8), (0, 0))), (DEPTH, 1, ROWS, WIDE))
+    back = exchange(jnp.concatenate([back, lum], axis=1).astype(f16), "depth")
+    sums = jnp.sum(back[:, 3, :8].astype(f32), axis=0)
+    sums = sums[:, :LANES] + sums[:, LANES:]
+    sums = exchange(jnp.broadcast_to(sums, (lax.axis_size("tile"), 8, LANES)), "tile")
     second = pl.pallas_call(
         back_kernel, in_specs=[smem, vmem, vmem], out_specs=vmem, out_shape=image, name="back"
-    )(background, front, back)
+    )(background, front, back[:, :3].astype(f32))
     pixels = ROWS * lax.axis_size("tile") * volume.shape[2]
     return pl.pallas_call(
         functools.partial(finish_kernel, float(pixels)),

time: 212 us -> 129 us (0.61)
  waiting for transfers between devices: 102 us -> 19.3 us
  between operations: 14.1 us -> 0.76 us
  starting transfers between devices: 19.6 us -> 29.1 us
    all_gather x1 -> x0, waiting for transfers between devices: 85.9 us -> none  [local(): sums = lax.all_gather(lum, ('tile', 'depth'), axis=0, tiled=False)]
    all_to_all x1 -> x2, starting transfers between devices: 8.3 us -> 17.9 us  [exchange(): return lax.all_to_all(part, axis, split_axis=0, concat_axis=0, tiled=True)]
    all_to_all x1 -> x2, waiting for transfers between devices: 11.4 us -> 14.9 us  [exchange(): return lax.all_to_all(part, axis, split_axis=0, concat_axis=0, tiled=True)]
    convert_element_type x4 -> x3, other arithmetic: 5.5 us -> 4.31 us  [the longest x2 3.27 us: local(): front = exchange(front.astype(f16), 'depth').astype(f32)]
  transfers between devices with their start and end apart: 6 -> 6, of which waited for: 4 -> 4; matrix products, arithmetic and copies ran while one was open for 2% -> 3% of each run, Pallas kernels for 1% -> 2%
where the time goes in v3:
time: 129 us; the launch traced here: 128 us
  Pallas kernels  49.9 us (39%)
  starting transfers between devices  29.1 us (23%)
  waiting for transfers between devices  19.3 us (15%)
  blocking collectives  13.1 us (10%)
  local copies, waits for them, and re-layouts  9.64 us (7%)
  other arithmetic  6.36 us (5%)
    pallas_call x1, Pallas kernels, march(): pl.pallas_call(march_kernel, grid=(steps,), in_specs=[smem, smem, smem, m...  44.2 us
    all_to_all x2, starting transfers between devices, exchange(): return lax.all_to_all(part, axis, split_axis=0, concat_axis=0, tiled=True)  17.9 us
    all_to_all x2, waiting for transfers between devices, exchange(): return lax.all_to_all(part, axis, split_axis=0, concat_axis=0, tiled=True)  14.9 us
    all_to_all x1, blocking collectives, exchange(): return lax.all_to_all(part, axis, split_axis=0, concat_axis=0, tiled=True)  13.1 us
    ppermute x2, starting transfers between devices, neighbours(): lax.ppermute(low_source, axis, forward)  8.06 us
    slice x1, local copies, waits for them, and re-layouts, local(): ylo, yhi = neighbours(volume[:, ROWS - 1], volume[:, 0], 'tile')  4.6 us
    ppermute x2, waiting for transfers between devices, neighbours(): lax.ppermute(high_source, axis, backward)  3.79 us
    unnamed x12, local copies, waits for them, and re-layouts  3.4 us
  transfers between devices with their start and end apart: 6, of which 4 were waited for; matrix products, arithmetic and copies ran while one was open for 3% of the time, Pallas kernels for 2%

profile of v3, /device:TPU:1, one launch (start us, length us, event | category | flops | bytes accessed | tf_op | source)
XLA Modules:
  0.0 128.3 jit_solution(17172143900793855626)
XLA Ops:
  0.0 4.6 %fusion = (bf16[64,1,4096]{2,1,0:T(2,128)(2,1)S(1)}, bf16[64,1,4096]{2,1,0:T(2,128)(2,1)S(1)}) fusion(bf16[64,16,4096]{2,1,0:T(8,128)(2,1)} %after_ref.1), kind=kLoop, calls=%fused_computation.9 | loop fusion | bytes 2097152 | tf_op jit(solution)/shard_map/slice | solution.py:296
  4.6 0.6 copy.16
  5.2 4.9 %collective-permute-start.2 = (bf16[64,4096]{1,0:T(8,128)(2,1)S(1)}, bf16[64,4096]{1,0:T(8,128)(2,1)S(1)}, u32[]{:S(2)}, u32[]{:S(2)}) collective-permute-start(bf16[64,4096]{1,0:T(8,128)(2,1)S(1)} %bitcast.10), channel_id=1, source_target_pairs={{0,16},{16,32},{32,48},{48,64},{64,80},{80,96},{96,112},{112,128},... | collective-permute-start | bytes 1572872 | tf_op jit(solution)/shard_map/ppermute | solution.py:288
  10.1 0.6 copy.15
  10.7 1.9 %collective-permute-start.3 = (bf16[64,4096]{1,0:T(8,128)(2,1)S(1)}, bf16[64,4096]{1,0:T(8,128)(2,1)S(1)}, u32[]{:S(2)}, u32[]{:S(2)}) collective-permute-start(bf16[64,4096]{1,0:T(8,128)(2,1)S(1)} %bitcast.11), channel_id=1, source_target_pairs={{16,0},{32,16},{48,32},{64,48},{80,64},{96,80},{112,96},{128,112},... | collective-permute-start | bytes 1572872 | tf_op jit(solution)/shard_map/ppermute | solution.py:288
  12.6 1.0 slice_bitcast_fusion
  13.6 3.1 %collective-permute-start = (bf16[16,4096]{1,0:T(8,128)(2,1)S(1)}, bf16[16,4096]{1,0:T(8,128)(2,1)S(1)}, u32[]{:S(2)}, u32[]{:S(2)}) collective-permute-start(bf16[16,4096]{1,0:T(8,128)(2,1)S(1)} %get-tuple-element.16), channel_id=1, source_target_pairs={{0,1},{1,2},{2,3},{3,4},{4,5},{5,6},{6,7},{7,8},{8,9},{9,10},{10,1... | collective-permute-start | bytes 393224 | tf_op jit(solution)/shard_map/ppermute | solution.py:288
  16.8 1.3 %collective-permute-start.1 = (bf16[16,4096]{1,0:T(8,128)(2,1)S(1)}, bf16[16,4096]{1,0:T(8,128)(2,1)S(1)}, u32[]{:S(2)}, u32[]{:S(2)}) collective-permute-start(bf16[16,4096]{1,0:T(8,128)(2,1)S(1)} %get-tuple-element.15), channel_id=1, source_target_pairs={{1,0},{2,1},{3,2},{4,3},{5,4},{6,5},{7,6},{8,7},{9,8},{10,9},{11,1... | collective-permute-start | bytes 393224 | tf_op jit(solution)/shard_map/ppermute | solution.py:288
  18.1 0.6 collective-permute-done.zlo_ref
  18.7 0.0 copy-start.3
  18.7 3.8 %collective-permute-done.1.zhi_ref = bf16[16,4096]{1,0:T(8,128)(2,1)S(1)} collective-permute-done((bf16[16,4096]{1,0:T(8,128)(2,1)S(1)}, bf16[16,4096]{1,0:T(8,128)(2,1)S(1)}, u32[]{:S(2)}, u32[]{:S(2)}) %collective-permute-start.1) | collective-permute-done | bytes 131104 | tf_op jit(solution)/shard_map/ppermute | solution.py:288
  22.5 0.0 copy-start.4
  22.5 0.0 collective-permute-done.2.ylo_ref.ylon_ref
  22.5 0.0 copy-start
  22.5 0.0 collective-permute-done.3.yhi_ref.yhin_ref
  22.5 0.0 copy-done.3
  22.5 0.6 copy-done.4
  23.1 0.2 copy-done
  23.3 0.0 copy-start.1
  23.3 0.8 copy-done.1
  24.1 44.2 %march.1 = (f32[16,4,16,256]{3,2,1,0:T(8,128)}, f32[16,3,16,256]{3,2,1,0:T(8,128)}) custom-call(f32[3]{0:T(128)} %light_ref.1, f32[3,16]{1,0:T(4,128)} %color_ref.1, f32[16]{0:T(128)} %opacity_ref.1, bf16[3,512,256]{2,1,0:T(8,128)(2,1)} %constant.8.clone.sxf_ref.sx_ref.sxl_ref, bf16[3,512,256]{2,1,0:T(8,128)(2,1)} %constant.8.clone.sxf_ref.sx_ref.sxl_ref, ...), custom_call_target="tpu_custom_call" | custom-call | flops 400000000 | bytes 24000000 | tf_op jit(solution)/shard_map/march/pallas_call | solution.py:202
  68.3 2.2 %convert_element_type.16 = f16[16,4,16,256]{3,2,1,0:T(8,128)(2,1)} convert(f32[16,4,16,256]{3,2,1,0:T(8,128)} %get-tuple-element.10) | non-fusion elementwise | flops 262144 | bytes 1572864 | tf_op jit(solution)/shard_map/convert_element_type | solution.py:302
  70.4 8.3 %all-to-all-start = ((f16[16,4,16,256]{3,2,1,0:T(8,128)(2,1)}), f16[16,4,16,256]{3,2,1,0:T(8,128)(2,1)S(1)}, u32[]{:S(2)}, u32[]{:S(2)}) async-start(f16[16,4,16,256]{3,2,1,0:T(8,128)(2,1)} %convert_element_type.16), calls=%async_computation | async-start | bytes 1048576 | tf_op jit(solution)/shard_map/all_to_all | solution.py:292
  79.4 1.2 convert.7
  80.6 10.3 %all-to-all-done = f16[16,4,16,256]{3,2,1,0:T(8,128)(2,1)S(1)} async-done(((f16[16,4,16,256]{3,2,1,0:T(8,128)(2,1)}), f16[16,4,16,256]{3,2,1,0:T(8,128)(2,1)S(1)}, u32[]{:S(2)}, u32[]{:S(2)}) %all-to-all-start) | async-done | bytes 524320 | tf_op jit(solution)/shard_map/all_to_all | solution.py:292
  90.9 1.1 convert_element_type.17.s_ref.f_ref
  92.0 1.9 %front.1 = (f32[3,16,256]{2,1,0:T(8,128)}, f32[8,256]{1,0:T(8,128)}) custom-call(f32[3]{0:T(128)} %bg_ref.3, f32[1]{0:T(128)S(6)} %copy.17.prior_ref, f32[16,4,16,256]{3,2,1,0:T(8,128)} %convert_element_type.17.s_ref.f_ref), custom_call_target="tpu_custom_call" | custom-call | tf_op jit(solution)/shard_map/front/pallas_call | solution.py:303
  94.0 0.7 pad_convert_fusion
  94.7 0.1 pad_maximum_fusion
  94.8 13.1 %all_to_all.15 = f16[16,4,16,256]{3,2,1,0:T(8,128)(2,1)S(1)} all-to-all(f16[16,4,16,256]{3,2,1,0:T(8,128)(2,1)S(1)} %pad_maximum_fusion), channel_id=1, replica_groups=mesh['tile'=16,'depth'=16] {'depth'}, dimensions={0} | all-to-all | bytes 1048576 | tf_op jit(solution)/shard_map/all_to_all | solution.py:292
  108.0 0.6 broadcast_in_dim.7
  108.6 9.6 %all-to-all-start.2 = ((f32[16,8,128]{2,1,0:T(8,128)}), f32[16,8,128]{2,1,0:T(8,128)S(1)}, u32[]{:S(2)}, u32[]{:S(2)}) async-start(f32[16,8,128]{2,1,0:T(8,128)} %broadcast_in_dim.7), calls=%async_computation.2 | async-start | bytes 131072 | tf_op jit(solution)/shard_map/all_to_all | solution.py:292
  118.2 1.0 slice_convert_fusion.s_ref
  119.2 2.2 %back.1.second_ref = f32[3,16,256]{2,1,0:T(8,128)} custom-call(f32[3]{0:T(128)} %bg_ref.3, f32[16,4,16,256]{3,2,1,0:T(8,128)} %convert_element_type.17.s_ref.f_ref, f32[16,3,16,256]{3,2,1,0:T(8,128)} %slice_convert_fusion.s_ref), custom_call_target="tpu_custom_call" | custom-call | tf_op jit(solution)/shard_map/back/pallas_call | solution.py:315
  121.4 4.6 %all-to-all-done.2.lum_ref = f32[16,8,128]{2,1,0:T(8,128)S(1)} async-done(((f32[16,8,128]{2,1,0:T(8,128)}), f32[16,8,128]{2,1,0:T(8,128)S(1)}, u32[]{:S(2)}, u32[]{:S(2)}) %all-to-all-start.2) | async-done | bytes 65568 | tf_op jit(solution)/shard_map/all_to_all | solution.py:292
  126.0 0.0 copy-start.2
  126.0 0.6 copy-done.2
  126.6 1.7 %finish.1 = f32[2,3,16,256]{3,2,1,0:T(8,128)} custom-call(f32[16,8,128]{2,1,0:T(8,128)} %copy-done.2, f32[3,16,256]{2,1,0:T(8,128)} %get-tuple-element.12.mapped_ref, f32[3,16,256]{2,1,0:T(8,128)} %back.1.second_ref), custom_call_target="tpu_custom_call" | custom-call | tf_op jit(solution)/shard_map/finish/pallas_call | solution.py:319
  (3 shorter events, 0.0 us)
Async XLA Ops:
  5.2 17.3 %collective-permute-start.2 = (bf16[64,4096]{1,0:T(8,128)(2,1)S(1)}, bf16[64,4096]{1,0:T(8,128)(2,1)S(1)}, u32[]{:S(2)}, u32[]{:S(2)}) collective-permute-start(bf16[64,4096]{1,0:T(8,128)(2,1)S(1)} %bitcast.10), channel_id=1, source_target_pairs={{0,16},{16,32},{32,48},{48,64},{64,80},{80,96},{96,112},{112,128},... | collective-permute-start | bytes 1572872 | tf_op jit(solution)/shard_map/ppermute | solution.py:288
  10.7 11.8 %collective-permute-start.3 = (bf16[64,4096]{1,0:T(8,128)(2,1)S(1)}, bf16[64,4096]{1,0:T(8,128)(2,1)S(1)}, u32[]{:S(2)}, u32[]{:S(2)}) collective-permute-start(bf16[64,4096]{1,0:T(8,128)(2,1)S(1)} %bitcast.11), channel_id=1, source_target_pairs={{16,0},{32,16},{48,32},{64,48},{80,64},{96,80},{112,96},{128,112},... | collective-permute-start | bytes 1572872 | tf_op jit(solution)/shard_map/ppermute | solution.py:288
  13.6 5.1 %collective-permute-start = (bf16[16,4096]{1,0:T(8,128)(2,1)S(1)}, bf16[16,4096]{1,0:T(8,128)(2,1)S(1)}, u32[]{:S(2)}, u32[]{:S(2)}) collective-permute-start(bf16[16,4096]{1,0:T(8,128)(2,1)S(1)} %get-tuple-element.16), channel_id=1, source_target_pairs={{0,1},{1,2},{2,3},{3,4},{4,5},{5,6},{6,7},{7,8},{8,9},{9,10},{10,1... | collective-permute-start | bytes 393224 | tf_op jit(solution)/shard_map/ppermute | solution.py:288
  16.8 5.7 %collective-permute-start.1 = (bf16[16,4096]{1,0:T(8,128)(2,1)S(1)}, bf16[16,4096]{1,0:T(8,128)(2,1)S(1)}, u32[]{:S(2)}, u32[]{:S(2)}) collective-permute-start(bf16[16,4096]{1,0:T(8,128)(2,1)S(1)} %get-tuple-element.15), channel_id=1, source_target_pairs={{1,0},{2,1},{3,2},{4,3},{5,4},{6,5},{7,6},{8,7},{9,8},{10,9},{11,1... | collective-permute-start | bytes 393224 | tf_op jit(solution)/shard_map/ppermute | solution.py:288
  18.7 3.8 %copy-start.3 = (bf16[16,4096]{1,0:T(8,128)(2,1)}, bf16[16,4096]{1,0:T(8,128)(2,1)S(1)}, u32[]{:S(2)}) copy-start(bf16[16,4096]{1,0:T(8,128)(2,1)S(1)} %collective-permute-done.zlo_ref) | copy-start | bytes 393220
  22.5 0.6 copy-start.4
  22.5 0.8 copy-start
  23.3 0.8 copy-start.1
  70.4 20.4 %all-to-all-start = ((f16[16,4,16,256]{3,2,1,0:T(8,128)(2,1)}), f16[16,4,16,256]{3,2,1,0:T(8,128)(2,1)S(1)}, u32[]{:S(2)}, u32[]{:S(2)}) async-start(f16[16,4,16,256]{3,2,1,0:T(8,128)(2,1)} %convert_element_type.16), calls=%async_computation | async-start | bytes 1048576 | tf_op jit(solution)/shard_map/all_to_all | solution.py:292
  108.6 17.4 %all-to-all-start.2 = ((f32[16,8,128]{2,1,0:T(8,128)}), f32[16,8,128]{2,1,0:T(8,128)S(1)}, u32[]{:S(2)}, u32[]{:S(2)}) async-start(f32[16,8,128]{2,1,0:T(8,128)} %broadcast_in_dim.7), calls=%async_computation.2 | async-start | bytes 131072 | tf_op jit(solution)/shard_map/all_to_all | solution.py:292
  126.0 0.6 copy-start.2

commit v4 on v3

--- a/solution.py
+++ b/solution.py
@@ -27,7 +27,8 @@
 DEPTH = 16
 WIDE = 256
 KNOTS = 16
-VMEM = 58 * 1024 * 1024
+VMEM = 50 * 1024 * 1024
+SMALL = 16 * 1024 * 1024
 
 
 def difference_matrices():
@@ -49,8 +50,19 @@
     return jnp.asarray(np.stack([first, base, last]), bf16), jnp.asarray(sy, bf16)
 
 
+COLUMNWISE = lax.GatherDimensionNumbers(
+    offset_dims=(),
+    collapsed_slice_dims=(0,),
+    start_index_map=(0,),
+    operand_batching_dims=(1,),
+    start_indices_batching_dims=(1,),
+)
+
+
 def pick(table, index):
-    return jnp.take_along_axis(table, index, axis=0, mode="promise_in_bounds")
+    return lax.gather(
+        table, index[:, :, None], COLUMNWISE, (1, 1), mode=lax.GatherScatterMode.PROMISE_IN_BOUNDS
+    )
 
 
 def halves(x):
@@ -108,10 +120,10 @@
             for j in range(8):
                 mid = f[2 * j + 1]
                 rise = f[2 * j + 2] - mid if j < 7 else 0.0
-                for row, value in ((k, mid), (4 + k, mid - f[2 * j]), (8 + k, rise)):
+                for row, value in ((k, mid), (4 + k, 2.0 * (mid - f[2 * j])), (8 + k, 2.0 * rise)):
                     table[8 * row + j : 8 * row + j + 1, :] = jnp.full((1, LANES), value, f32)
         for j in range(8):
-            table[96 + j : 97 + j, :] = jnp.full((1, LANES), 2.0 * j + 1.0, f32)
+            table[96 + j : 97 + j, :] = jnp.full((1, LANES), j + 0.5, f32)
         for g in range(4):
             for part in range(2):
                 differences(g, part, *first)
@@ -119,12 +131,13 @@
     tb = [table[8 * k : 8 * k + 8, :] for k in range(13)]
 
     def sample(below, v, above, dx, dy, state):
+        v = v * 7.5
         dz = above - below
         q = (dz * dz + 0.16) + (dy * dy + dx * dx)
         dot = (dz * lz + dy * ly) + dx * lx
         shade = (AMBIENT + 0.5 * (1.0 - AMBIENT)) + dot * lax.rsqrt(q)
-        j = (v * 7.5).astype(jnp.int32)
-        u = v * 15.0 - pick(tb[12], j)
+        j = v.astype(jnp.int32)
+        u = v - pick(tb[12], j)
         left = u < 0.0
         alpha, red, green, blue = [
             pick(tb[k], j) + jnp.where(left, pick(tb[4 + k], j), pick(tb[8 + k], j)) * u
@@ -238,6 +251,40 @@
     )
 
 
+def edges_kernel(pick_ref, v_ref, zlast_ref, zfirst_ref, ylast_ref, yfirst_ref):
+    zlast_ref[...] = v_ref[PLANES - 1]
+    zfirst_ref[...] = v_ref[0]
+    width = v_ref.shape[2]
+    for g in range(4):
+        planes = slice(16 * g, 16 * g + 16)
+        rows = v_ref[planes].reshape(256, width)
+        rows = jnp.dot(pick_ref[...], rows, preferred_element_type=f32).astype(bf16)
+        ylast_ref[planes, :] = rows[:16]
+        yfirst_ref[planes, :] = rows[16:]
+
+
+def edges(vol):
+    width = 2048
+    choose = np.zeros((32, 256), np.float32)
+    for p in range(16):
+        choose[p, ROWS * p + ROWS - 1] = 1
+        choose[16 + p, ROWS * p] = 1
+    return pl.pallas_call(
+        edges_kernel,
+        grid=(vol.shape[2] // width,),
+        in_specs=[
+            pl.BlockSpec((32, 256), lambda s: (0, 0)),
+            pl.BlockSpec((PLANES, ROWS, width), lambda s: (0, 0, s)),
+        ],
+        out_specs=[pl.BlockSpec((n, width), lambda s: (0, s)) for n in (ROWS, ROWS, PLANES, PLANES)],
+        out_shape=[
+            jax.ShapeDtypeStruct((n, vol.shape[2]), bf16) for n in (ROWS, ROWS, PLANES, PLANES)
+        ],
+        compiler_params=pltpu.CompilerParams(vmem_limit_bytes=58 * 1024 * 1024),
+        name="edges",
+    )(jnp.asarray(choose, bf16), vol)
+
+
 def front_kernel(bg_ref, prior_ref, s_ref, mapped_ref, lum_ref):
     total = jnp.zeros((8, LANES), f32)
     for c in range(2):
@@ -293,8 +340,9 @@
 
 
 def local(volume, tf_color, tf_opacity, light, background, exposure_prior):
-    ylo, yhi = neighbours(volume[:, ROWS - 1], volume[:, 0], "tile")
-    zlo, zhi = neighbours(volume[PLANES - 1], volume[0], "depth")
+    zlast, zfirst, ylast, yfirst = edges(volume)
+    ylo, yhi = neighbours(ylast, yfirst, "tile")
+    zlo, zhi = neighbours(zlast, zfirst, "depth")
     front, back = march(volume, zlo, zhi, ylo, yhi, light, tf_color, tf_opacity)
     smem = pl.BlockSpec(memory_space=pltpu.SMEM)
     vmem = pl.BlockSpec(memory_space=pltpu.VMEM)
@@ -305,6 +353,7 @@
         in_specs=[smem, smem, vmem],
         out_specs=[vmem] * 2,
         out_shape=[image, jax.ShapeDtypeStruct((8, WIDE), f32)],
+        compiler_params=pltpu.CompilerParams(vmem_limit_bytes=SMALL),
         name="front",
     )(background, exposure_prior, front)
     lum = jnp.broadcast_to(jnp.pad(lum, ((0, 8), (0, 0))), (DEPTH, 1, ROWS, WIDE))
@@ -313,7 +362,12 @@
     sums = sums[:, :LANES] + sums[:, LANES:]
     sums = exchange(jnp.broadcast_to(sums, (lax.axis_size("tile"), 8, LANES)), "tile")
     second = pl.pallas_call(
-        back_kernel, in_specs=[smem, vmem, vmem], out_specs=vmem, out_shape=image, name="back"
+        back_kernel,
+        in_specs=[smem, vmem, vmem],
+        out_specs=vmem,
+        out_shape=image,
+        compiler_params=pltpu.CompilerParams(vmem_limit_bytes=SMALL),
+        name="back",
     )(background, front, back[:, :3].astype(f32))
     pixels = ROWS * lax.axis_size("tile") * volume.shape[2]
     return pl.pallas_call(
@@ -321,6 +375,7 @@
         in_specs=[vmem] * 3,
         out_specs=vmem,
         out_shape=jax.ShapeDtypeStruct((2, 3, ROWS, WIDE), f32),
+        compiler_params=pltpu.CompilerParams(vmem_limit_bytes=SMALL),
         name="finish",
     )(sums, mapped, second)
 

time: 129 us -> 117 us (0.907)
  local copies, waits for them, and re-layouts: 9.64 us -> 0.68 us
  other arithmetic: 6.36 us -> 1.36 us
  waiting for transfers between devices: 19.3 us -> 23.1 us
  Pallas kernels: 49.9 us -> 48.5 us
    pallas_call x0 -> x1, Pallas kernels: none -> 5.22 us  [edges(): pl.pallas_call(edges_kernel, grid=(vol.shape[2] // width,), in_specs=[pl....]
    slice x1 -> x0, local copies, waits for them, and re-layouts: 4.6 us -> none  [local(): ylo, yhi = neighbours(volume[:, ROWS - 1], volume[:, 0], 'tile')]
    all_to_all x2, waiting for transfers between devices: 14.9 us -> 18.5 us  [exchange(): return lax.all_to_all(part, axis, split_axis=0, concat_axis=0, tiled=True)]
    unnamed x12, local copies, waits for them, and re-layouts: 3.4 us -> 0.03 us
    pallas_call x1, Pallas kernels: 44.2 us -> 41.2 us  [march(): pl.pallas_call(march_kernel, grid=(steps,), in_specs=[smem, smem, smem, m...]
    convert_element_type x2, other arithmetic: 3.27 us -> 1.05 us  [local(): front = exchange(front.astype(f16), 'depth').astype(f32)]
    another operation x2, other arithmetic: 1.9 us -> 0.08 us
    pallas_call x1, Pallas kernels: 2.16 us -> 0.63 us  [local(): pl.pallas_call(back_kernel, in_specs=[smem, vmem, vmem], out_specs=vmem,...]
  transfers between devices with their start and end apart: 6 -> 6, of which waited for: 4 -> 4; matrix products, arithmetic and copies ran while one was open for 3% -> 0% of each run, Pallas kernels for 2% -> 1%
where the time goes in v4:
time: 117 us
  Pallas kernels  48.5 us (41%)
  starting transfers between devices  29.1 us (25%)
  waiting for transfers between devices  23.1 us (20%)
  blocking collectives  13.1 us (11%)
  other arithmetic  1.36 us (1%)
    pallas_call x1, Pallas kernels, march(): pl.pallas_call(march_kernel, grid=(steps,), in_specs=[smem, smem, smem, m...  41.2 us
    all_to_all x2, waiting for transfers between devices, exchange(): return lax.all_to_all(part, axis, split_axis=0, concat_axis=0, tiled=True)  18.5 us
    all_to_all x2, starting transfers between devices, exchange(): return lax.all_to_all(part, axis, split_axis=0, concat_axis=0, tiled=True)  17.9 us
    all_to_all x1, blocking collectives, exchange(): return lax.all_to_all(part, axis, split_axis=0, concat_axis=0, tiled=True)  13.1 us
    ppermute x2, starting transfers between devices, neighbours(): lax.ppermute(low_source, axis, forward)  8.04 us
    pallas_call x1, Pallas kernels, edges(): pl.pallas_call(edges_kernel, grid=(vol.shape[2] // width,), in_specs=[pl....  5.22 us
    ppermute x2, waiting for transfers between devices, neighbours(): lax.ppermute(high_source, axis, backward)  3.7 us
    ppermute x2, starting transfers between devices, neighbours(): lax.ppermute(high_source, axis, backward)  3.21 us
  transfers between devices with their start and end apart: 6, of which 4 were waited for; matrix products, arithmetic and copies ran while one was open for 0% of the time, Pallas kernels for 1%

profile of v4, /device:TPU:1, one launch (start us, length us, event | category | flops | bytes accessed | tf_op | source)
XLA Modules:
  0.0 116.7 jit_solution(5652885326649176187)
XLA Ops:
  0.0 0.0 copy-start
  0.0 0.0 copy-start.1
  0.0 0.0 copy-start.2
  0.0 0.0 copy-start.5
  0.0 0.0 copy-start.4
  0.0 5.2 %edges.1 = (bf16[16,4096]{1,0:T(8,128)(2,1)}, bf16[16,4096]{1,0:T(8,128)(2,1)}, bf16[64,4096]{1,0:T(8,128)(2,1)}, bf16[64,4096]{1,0:T(8,128)(2,1)}) custom-call(bf16[32,256]{1,0:T(8,128)(2,1)} %constant.10.clone.pick_ref, bf16[64,16,4096]{2,1,0:T(8,128)(2,1)} %after_ref.1), custom_call_target="tpu_custom_call" | custom-call | tf_op jit(solution)/shard_map/edges/pallas_call | solution.py:272
  5.2 4.9 %collective-permute-start.2 = (bf16[64,4096]{1,0:T(8,128)(2,1)}, bf16[64,4096]{1,0:T(8,128)(2,1)S(1)}, u32[]{:S(2)}, u32[]{:S(2)}) collective-permute-start(bf16[64,4096]{1,0:T(8,128)(2,1)} %get-tuple-element.15), channel_id=1, source_target_pairs={{0,16},{16,32},{32,48},{48,64},{64,80},{80,96},{96,112},{112,128},... | collective-permute-start | bytes 1572872 | tf_op jit(solution)/shard_map/ppermute | solution.py:335
  10.2 1.9 %collective-permute-start.3 = (bf16[64,4096]{1,0:T(8,128)(2,1)}, bf16[64,4096]{1,0:T(8,128)(2,1)S(1)}, u32[]{:S(2)}, u32[]{:S(2)}) collective-permute-start(bf16[64,4096]{1,0:T(8,128)(2,1)} %get-tuple-element.16), channel_id=1, source_target_pairs={{16,0},{32,16},{48,32},{64,48},{80,64},{96,80},{112,96},{128,112},... | collective-permute-start | bytes 1572872 | tf_op jit(solution)/shard_map/ppermute | solution.py:335
  12.1 3.1 %collective-permute-start = (bf16[16,4096]{1,0:T(8,128)(2,1)}, bf16[16,4096]{1,0:T(8,128)(2,1)S(1)}, u32[]{:S(2)}, u32[]{:S(2)}) collective-permute-start(bf16[16,4096]{1,0:T(8,128)(2,1)} %get-tuple-element.13), channel_id=1, source_target_pairs={{0,1},{1,2},{2,3},{3,4},{4,5},{5,6},{6,7},{7,8},{8,9},{9,10},{10,1... | collective-permute-start | bytes 393224 | tf_op jit(solution)/shard_map/ppermute | solution.py:335
  15.2 0.0 copy-start.3
  15.2 1.3 %collective-permute-start.1 = (bf16[16,4096]{1,0:T(8,128)(2,1)}, bf16[16,4096]{1,0:T(8,128)(2,1)S(1)}, u32[]{:S(2)}, u32[]{:S(2)}) collective-permute-start(bf16[16,4096]{1,0:T(8,128)(2,1)} %get-tuple-element.14), channel_id=1, source_target_pairs={{1,0},{2,1},{3,2},{4,3},{5,4},{6,5},{7,6},{8,7},{9,8},{10,9},{11,1... | collective-permute-start | bytes 393224 | tf_op jit(solution)/shard_map/ppermute | solution.py:335
  16.5 0.9 collective-permute-done.zlo_ref
  17.5 3.7 %collective-permute-done.1.zhi_ref = bf16[16,4096]{1,0:T(8,128)(2,1)S(1)} collective-permute-done((bf16[16,4096]{1,0:T(8,128)(2,1)}, bf16[16,4096]{1,0:T(8,128)(2,1)S(1)}, u32[]{:S(2)}, u32[]{:S(2)}) %collective-permute-start.1) | collective-permute-done | bytes 131104 | tf_op jit(solution)/shard_map/ppermute | solution.py:335
  21.2 0.0 collective-permute-done.2.ylo_ref.ylon_ref
  21.2 0.0 collective-permute-done.3.yhi_ref.yhin_ref
  21.2 0.0 copy-done
  21.2 0.0 copy-done.1
  21.2 0.0 copy-done.2
  21.2 0.0 copy-done.5
  21.2 0.0 copy-done.4
  21.2 41.2 %march.1 = (f32[16,4,16,256]{3,2,1,0:T(8,128)S(1)}, f32[16,3,16,256]{3,2,1,0:T(8,128)S(1)}) custom-call(f32[3]{0:T(128)S(1)} %copy-done.4, f32[3,16]{1,0:T(4,128)S(1)} %copy-done.2, f32[16]{0:T(128)S(1)} %copy-done.5, bf16[3,512,256]{2,1,0:T(8,128)(2,1)S(1)} %copy-done, bf16[3,512,256]{2,1,0:T(8,128)(2,1)S(1)} %copy-done, bf16[3,512,256]{2,1,0:T(8,128)(2,1)S(1)} %copy-done, ...), custom_call_target="tpu_custom_call" | custom-call | flops 400000000 | bytes 24000000 | tf_op jit(solution)/shard_map/march/pallas_call | solution.py:215
  62.4 0.9 convert_element_type.16
  63.4 8.3 %all-to-all-start = ((f16[16,4,16,256]{3,2,1,0:T(8,128)(2,1)}), f16[16,4,16,256]{3,2,1,0:T(8,128)(2,1)S(1)}, u32[]{:S(2)}, u32[]{:S(2)}) async-start(f16[16,4,16,256]{3,2,1,0:T(8,128)(2,1)} %convert_element_type.16), calls=%async_computation | async-start | bytes 1048576 | tf_op jit(solution)/shard_map/all_to_all | solution.py:339
  72.3 0.1 convert.7
  72.4 11.4 %all-to-all-done = f16[16,4,16,256]{3,2,1,0:T(8,128)(2,1)S(1)} async-done(((f16[16,4,16,256]{3,2,1,0:T(8,128)(2,1)}), f16[16,4,16,256]{3,2,1,0:T(8,128)(2,1)S(1)}, u32[]{:S(2)}, u32[]{:S(2)}) %all-to-all-start) | async-done | bytes 524320 | tf_op jit(solution)/shard_map/all_to_all | solution.py:339
  83.8 0.1 convert_element_type.17.s_ref.f_ref
  83.9 0.0 copy-done.3
  83.9 0.7 front.1
  84.6 0.1 pad_maximum_fusion
  84.8 13.1 %all_to_all.15 = f16[16,4,16,256]{3,2,1,0:T(8,128)(2,1)S(1)} all-to-all(f16[16,4,16,256]{3,2,1,0:T(8,128)(2,1)S(1)} %pad_maximum_fusion), channel_id=1, replica_groups=mesh['tile'=16,'depth'=16] {'depth'}, dimensions={0} | all-to-all | bytes 1048576 | tf_op jit(solution)/shard_map/all_to_all | solution.py:339
  97.9 0.6 broadcast_in_dim.7
  98.6 9.6 %all-to-all-start.2 = ((f32[16,8,128]{2,1,0:T(8,128)}), f32[16,8,128]{2,1,0:T(8,128)S(1)}, u32[]{:S(2)}, u32[]{:S(2)}) async-start(f32[16,8,128]{2,1,0:T(8,128)} %broadcast_in_dim.7), calls=%async_computation.2 | async-start | bytes 131072 | tf_op jit(solution)/shard_map/all_to_all | solution.py:339
  108.1 0.1 slice_convert_fusion.s_ref
  108.2 0.6 back.1.second_ref
  108.9 7.1 %all-to-all-done.2.lum_ref = f32[16,8,128]{2,1,0:T(8,128)S(1)} async-done(((f32[16,8,128]{2,1,0:T(8,128)}), f32[16,8,128]{2,1,0:T(8,128)S(1)}, u32[]{:S(2)}, u32[]{:S(2)}) %all-to-all-start.2) | async-done | bytes 65568 | tf_op jit(solution)/shard_map/all_to_all | solution.py:339
  115.9 0.8 finish.1
  (4 shorter events, 0.0 us)
Async XLA Ops:
  0.0 21.2 %copy-start = (bf16[3,512,256]{2,1,0:T(8,128)(2,1)S(1)}, bf16[3,512,256]{2,1,0:T(8,128)(2,1)}, u32[]{:S(2)}) copy-start(bf16[3,512,256]{2,1,0:T(8,128)(2,1)} %constant.11.clone.sxf_ref.sx_ref.sxl_ref) | copy-start | bytes 2359300
  0.0 21.2 %copy-start.1 = (bf16[2,128,256]{2,1,0:T(8,128)(2,1)S(1)}, bf16[2,128,256]{2,1,0:T(8,128)(2,1)}, u32[]{:S(2)}) copy-start(bf16[2,128,256]{2,1,0:T(8,128)(2,1)} %constant.12.clone.sy_ref) | copy-start | bytes 393220
  0.0 21.2 %copy-start.2 = (f32[3,16]{1,0:T(4,128)S(1)}, f32[3,16]{1,0:T(4,128)}, u32[]{:S(2)}) copy-start(f32[3,16]{1,0:T(4,128)} %color_ref.1) | copy-start | bytes 580
  0.0 21.2 %copy-start.5 = (f32[16]{0:T(128)S(1)}, f32[16]{0:T(128)}, u32[]{:S(2)}) copy-start(f32[16]{0:T(128)} %opacity_ref.1) | copy-start | bytes 196
  0.0 21.2 %copy-start.4 = (f32[3]{0:T(128)S(1)}, f32[3]{0:T(128)}, u32[]{:S(2)}) copy-start(f32[3]{0:T(128)} %light_ref.1) | copy-start | bytes 40
  5.2 15.9 %collective-permute-start.2 = (bf16[64,4096]{1,0:T(8,128)(2,1)}, bf16[64,4096]{1,0:T(8,128)(2,1)S(1)}, u32[]{:S(2)}, u32[]{:S(2)}) collective-permute-start(bf16[64,4096]{1,0:T(8,128)(2,1)} %get-tuple-element.15), channel_id=1, source_target_pairs={{0,16},{16,32},{32,48},{48,64},{64,80},{80,96},{96,112},{112,128},... | collective-permute-start | bytes 1572872 | tf_op jit(solution)/shard_map/ppermute | solution.py:335
  10.2 11.0 %collective-permute-start.3 = (bf16[64,4096]{1,0:T(8,128)(2,1)}, bf16[64,4096]{1,0:T(8,128)(2,1)S(1)}, u32[]{:S(2)}, u32[]{:S(2)}) collective-permute-start(bf16[64,4096]{1,0:T(8,128)(2,1)} %get-tuple-element.16), channel_id=1, source_target_pairs={{16,0},{32,16},{48,32},{64,48},{80,64},{96,80},{112,96},{128,112},... | collective-permute-start | bytes 1572872 | tf_op jit(solution)/shard_map/ppermute | solution.py:335
  12.1 5.4 %collective-permute-start = (bf16[16,4096]{1,0:T(8,128)(2,1)}, bf16[16,4096]{1,0:T(8,128)(2,1)S(1)}, u32[]{:S(2)}, u32[]{:S(2)}) collective-permute-start(bf16[16,4096]{1,0:T(8,128)(2,1)} %get-tuple-element.13), channel_id=1, source_target_pairs={{0,1},{1,2},{2,3},{3,4},{4,5},{5,6},{6,7},{7,8},{8,9},{9,10},{10,1... | collective-permute-start | bytes 393224 | tf_op jit(solution)/shard_map/ppermute | solution.py:335
  15.2 68.7 %copy-start.3 = (f32[3]{0:T(128)S(1)}, f32[3]{0:T(128)}, u32[]{:S(2)}) copy-start(f32[3]{0:T(128)} %bg_ref.3) | copy-start | bytes 40
  15.2 5.9 %collective-permute-start.1 = (bf16[16,4096]{1,0:T(8,128)(2,1)}, bf16[16,4096]{1,0:T(8,128)(2,1)S(1)}, u32[]{:S(2)}, u32[]{:S(2)}) collective-permute-start(bf16[16,4096]{1,0:T(8,128)(2,1)} %get-tuple-element.14), channel_id=1, source_target_pairs={{1,0},{2,1},{3,2},{4,3},{5,4},{6,5},{7,6},{8,7},{9,8},{10,9},{11,1... | collective-permute-start | bytes 393224 | tf_op jit(solution)/shard_map/ppermute | solution.py:335
  63.4 20.4 %all-to-all-start = ((f16[16,4,16,256]{3,2,1,0:T(8,128)(2,1)}), f16[16,4,16,256]{3,2,1,0:T(8,128)(2,1)S(1)}, u32[]{:S(2)}, u32[]{:S(2)}) async-start(f16[16,4,16,256]{3,2,1,0:T(8,128)(2,1)} %convert_element_type.16), calls=%async_computation | async-start | bytes 1048576 | tf_op jit(solution)/shard_map/all_to_all | solution.py:339
  98.6 17.4 %all-to-all-start.2 = ((f32[16,8,128]{2,1,0:T(8,128)}), f32[16,8,128]{2,1,0:T(8,128)S(1)}, u32[]{:S(2)}, u32[]{:S(2)}) async-start(f32[16,8,128]{2,1,0:T(8,128)} %broadcast_in_dim.7), calls=%async_computation.2 | async-start | bytes 131072 | tf_op jit(solution)/shard_map/all_to_all | solution.py:339

commit v5 on v4

--- a/solution.py
+++ b/solution.py
@@ -40,13 +40,16 @@
     first[:LANES] = 0
     last = base.copy()
     last[LANES + WIDE :] = 0
-    sy = np.zeros((2, 128, WIDE), np.float32)
+    sy = np.zeros((2, 2, 128, WIDE), np.float32)
     for e in range(2):
         for p in range(8):
             for r in range(ROWS):
                 o = ROWS * p + r
-                sy[e, o, o - 1 if r > 0 else 128 + 8 * e + p] = -1
-                sy[e, o, o + 1 if r < ROWS - 1 else 144 + 8 * e + p] = 1
+                for odd in range(2):
+                    before = 144 - 16 * odd + 8 * e + p
+                    after = 128 + 16 * odd + 8 * e + p
+                    sy[odd, e, o, o - 1 if r > 0 else before] = -1
+                    sy[odd, e, o, o + 1 if r < ROWS - 1 else after] = 1
     return jnp.asarray(np.stack([first, base, last]), bf16), jnp.asarray(sy, bf16)
 
 
@@ -71,9 +74,9 @@
 
 
 def march_kernel(
-    light_ref, color_ref, opacity_ref, sxf_ref, sx_ref, sxl_ref, sy_ref,
+    odd_ref, light_ref, color_ref, opacity_ref, sxf_ref, sx_ref, sxl_ref, sy_ref,
     before_ref, cur_ref, next_ref, after_ref,
-    zlo_ref, zhi_ref, ylo_ref, yhi_ref, ylon_ref, yhin_ref,
+    za_ref, zb_ref, ya_ref, yb_ref, yan_ref, ybn_ref,
     front_ref, back_ref, dxa, dya, dxb, dyb, acc, table,
 ):
     s = pl.program_id(0)
@@ -97,20 +100,20 @@
                 some = pl.ds(pl.multiple_of(16 * g + 8 * e, 8), 8)
                 rows = pl.ds(pl.multiple_of(256 * g + 128 * e, 128), 128)
                 tall = jnp.concatenate([ref[some, :, cols].reshape(128, WIDE), *edges, fill], axis=0)
-                dy[rows, :] = jnp.dot(sy_ref[e], tall, preferred_element_type=f32)
+                dy[rows, :] = jnp.dot(sy_ref[odd_ref[0], e], tall, preferred_element_type=f32)
 
     low, high = slice(0, WIDE), slice(WIDE, 2 * WIDE)
     first = (
         [(before_ref, slice(0, 128)), (cur_ref, slice(0, 384))],
-        sxf_ref, (ylo_ref, low), (yhi_ref, low), (cur_ref, low), dxa, dya,
+        sxf_ref, (ya_ref, low), (yb_ref, low), (cur_ref, low), dxa, dya,
     )
     odd = (
         [(cur_ref, slice(128, 512)), (next_ref, slice(0, 128))],
-        sxl_ref, (ylo_ref, high), (yhi_ref, high), (cur_ref, high), dxb, dyb,
+        sxl_ref, (ya_ref, high), (yb_ref, high), (cur_ref, high), dxb, dyb,
     )
     even = (
         [(cur_ref, slice(384, 512)), (next_ref, low), (after_ref, slice(0, 128))],
-        sx_ref, (ylon_ref, low), (yhin_ref, low), (next_ref, low), dxa, dya,
+        sx_ref, (yan_ref, low), (ybn_ref, low), (next_ref, low), dxa, dya,
     )
 
     @pl.when(s == 0)
@@ -159,16 +162,16 @@
                 for i in range(7):
                     acc[side, h, i] = jnp.full((8, LANES), 1.0 if i == 3 else 0.0, f32)
 
-        def group(g, unused, half=half, dx=dx, dy=dy, following=following):
+        for g in range(4):
             for side in range(2):
                 differences(g, side, *following)
                 lanes = slice(LANES * side, LANES * side + LANES)
                 at = WIDE * half + LANES * side
                 cols = slice(at, at + LANES)
-                lo = jnp.where(g == 0, zlo_ref[:, cols], cur_ref[jnp.maximum(16 * g - 1, 0), :, cols])
-                hi = jnp.where(
-                    g == 3, zhi_ref[:, cols], cur_ref[jnp.minimum(16 * g + 16, PLANES - 1), :, cols]
-                )
+                ends = [za_ref[:, cols].astype(f32), zb_ref[:, cols].astype(f32)]
+                swap = odd_ref[1] == 1
+                lo = jnp.where(swap, *ends) if g == 0 else cur_ref[16 * g - 1, :, cols]
+                hi = jnp.where(swap, *ends[::-1]) if g == 3 else cur_ref[16 * g + 16, :, cols]
                 below, here = halves(lo), halves(cur_ref[16 * g, :, cols])
                 state = [[acc[side, h, i] for i in range(7)] for h in range(2)]
                 for p in range(16):
@@ -182,9 +185,7 @@
                 for h in range(2):
                     for i in range(7):
                         acc[side, h, i] = state[h][i]
-            return unused
-
-        lax.fori_loop(0, 4, group, 0, unroll=4)
+
         for side in range(2):
             lanes = slice(LANES * side, LANES * side + LANES)
             for h in range(2):
@@ -195,7 +196,7 @@
                 front_ref[half, 3, rows, lanes] = 1.0 - acc[side, h, 3]
 
 
-def march(vol, zlo, zhi, ylo, yhi, light, tf_color, tf_opacity):
+def march(vol, odd, za, zb, ya, yb, light, tf_color, tf_opacity):
     sx, sy = difference_matrices()
     steps = DEPTH // 2
 
@@ -219,10 +220,11 @@
             smem,
             smem,
             smem,
+            smem,
             matrix(lambda s: 0),
             matrix(lambda s: 1),
             matrix(lambda s: jnp.where(s == steps - 1, 2, 1)),
-            pl.BlockSpec((2, 128, WIDE), lambda s: (0, 0, 0)),
+            pl.BlockSpec((2, 2, 128, WIDE), lambda s: (0, 0, 0, 0)),
             block(LANES, lambda s: 0),
             block(2 * WIDE, lambda s: s),
             block(WIDE, follower),
@@ -246,34 +248,36 @@
         ),
         name="march",
     )(
-        light, tf_color, tf_opacity, sx, sx, sx, sy, vol, vol, vol, vol,
-        zlo, zhi, ylo, yhi, ylo, yhi,
-    )
-
-
-def edges_kernel(pick_ref, v_ref, zlast_ref, zfirst_ref, ylast_ref, yfirst_ref):
-    zlast_ref[...] = v_ref[PLANES - 1]
-    zfirst_ref[...] = v_ref[0]
+        odd, light, tf_color, tf_opacity, sx, sx, sx, sy, vol, vol, vol, vol,
+        za, zb, ya, yb, ya, yb,
+    )
+
+
+def edges_kernel(odd_ref, pick_ref, v_ref, za_ref, zb_ref, ya_ref, yb_ref):
+    za_ref[...] = v_ref[(PLANES - 1) * (1 - odd_ref[1])]
+    zb_ref[...] = v_ref[(PLANES - 1) * odd_ref[1]]
     width = v_ref.shape[2]
     for g in range(4):
         planes = slice(16 * g, 16 * g + 16)
         rows = v_ref[planes].reshape(256, width)
-        rows = jnp.dot(pick_ref[...], rows, preferred_element_type=f32).astype(bf16)
-        ylast_ref[planes, :] = rows[:16]
-        yfirst_ref[planes, :] = rows[16:]
-
-
-def edges(vol):
+        rows = jnp.dot(pick_ref[odd_ref[0]], rows, preferred_element_type=f32).astype(bf16)
+        ya_ref[planes, :] = rows[:16]
+        yb_ref[planes, :] = rows[16:]
+
+
+def edges(vol, odd):
     width = 2048
-    choose = np.zeros((32, 256), np.float32)
+    choose = np.zeros((2, 32, 256), np.float32)
     for p in range(16):
-        choose[p, ROWS * p + ROWS - 1] = 1
-        choose[16 + p, ROWS * p] = 1
+        for o in range(2):
+            choose[o, 16 * o + p, ROWS * p + ROWS - 1] = 1
+            choose[o, 16 - 16 * o + p, ROWS * p] = 1
     return pl.pallas_call(
         edges_kernel,
         grid=(vol.shape[2] // width,),
         in_specs=[
-            pl.BlockSpec((32, 256), lambda s: (0, 0)),
+            pl.BlockSpec(memory_space=pltpu.SMEM),
+            pl.BlockSpec((2, 32, 256), lambda s: (0, 0, 0)),
             pl.BlockSpec((PLANES, ROWS, width), lambda s: (0, 0, s)),
         ],
         out_specs=[pl.BlockSpec((n, width), lambda s: (0, s)) for n in (ROWS, ROWS, PLANES, PLANES)],
@@ -282,7 +286,7 @@
         ],
         compiler_params=pltpu.CompilerParams(vmem_limit_bytes=58 * 1024 * 1024),
         name="edges",
-    )(jnp.asarray(choose, bf16), vol)
+    )(odd, jnp.asarray(choose, bf16), vol)
 
 
 def front_kernel(bg_ref, prior_ref, s_ref, mapped_ref, lum_ref):
@@ -328,11 +332,11 @@
         o_ref[1, i] = scaled / (1.0 + scaled)
 
 
-def neighbours(low_source, high_source, axis):
+def swap(first, second, axis):
     count = lax.axis_size(axis)
-    forward = [(i, i + 1) for i in range(count - 1)]
-    backward = [(target, source) for source, target in forward]
-    return lax.ppermute(low_source, axis, forward), lax.ppermute(high_source, axis, backward)
+    pairs = [(i, i ^ 1) for i in range(count)]
+    others = [(i, i + 1 if i % 2 else i - 1) for i in range(1, count - 1)]
+    return lax.ppermute(first, axis, pairs), lax.ppermute(second, axis, others)
 
 
 def exchange(part, axis):
@@ -340,10 +344,11 @@
 
 
 def local(volume, tf_color, tf_opacity, light, background, exposure_prior):
-    zlast, zfirst, ylast, yfirst = edges(volume)
-    ylo, yhi = neighbours(ylast, yfirst, "tile")
-    zlo, zhi = neighbours(zlast, zfirst, "depth")
-    front, back = march(volume, zlo, zhi, ylo, yhi, light, tf_color, tf_opacity)
+    odd = jnp.stack([lax.axis_index(axis) % 2 for axis in ("tile", "depth")])
+    za, zb, ya, yb = edges(volume, odd)
+    ya, yb = swap(ya, yb, "tile")
+    za, zb = swap(za, zb, "depth")
+    front, back = march(volume, odd, za, zb, ya, yb, light, tf_color, tf_opacity)
     smem = pl.BlockSpec(memory_space=pltpu.SMEM)
     vmem = pl.BlockSpec(memory_space=pltpu.VMEM)
     image = jax.ShapeDtypeStruct((3, ROWS, WIDE), f32)

time: 117 us -> 116 us (level)
  starting transfers between devices: 29.1 us -> 23.9 us
  other arithmetic: 1.36 us -> 3.23 us
  waiting for transfers between devices: 23.1 us -> 24.5 us
    ppermute x4, starting transfers between devices: 11.3 us -> 7.02 us  [the longest x2 4.32 us: swap(): lax.ppermute(first, axis, pairs)]
    ppermute x4, waiting for transfers between devices: 4.63 us -> 6.88 us  [the longest x2 4.01 us: swap(): lax.ppermute(second, axis, others)]
    convert_element_type x2, other arithmetic: 1.05 us -> 2.31 us  [local(): front = exchange(front.astype(f16), 'depth').astype(f32)]
where the time goes in v5:
time: 116 us
  Pallas kernels  49.2 us (42%)
  waiting for transfers between devices  24.5 us (21%)
  starting transfers between devices  23.9 us (21%)
  blocking collectives  13.2 us (11%)
  other arithmetic  3.23 us (3%)
    pallas_call x1, Pallas kernels, march(): pl.pallas_call(march_kernel, grid=(steps,), in_specs=[smem, smem, smem, s...  42 us
    all_to_all x2, waiting for transfers between devices, exchange(): return lax.all_to_all(part, axis, split_axis=0, concat_axis=0, tiled=True)  17.6 us
    all_to_all x2, starting transfers between devices, exchange(): return lax.all_to_all(part, axis, split_axis=0, concat_axis=0, tiled=True)  16.9 us
    all_to_all x1, blocking collectives, exchange(): return lax.all_to_all(part, axis, split_axis=0, concat_axis=0, tiled=True)  13.2 us
    pallas_call x1, Pallas kernels, edges(): pl.pallas_call(edges_kernel, grid=(vol.shape[2] // width,), in_specs=[pl....  5.13 us
    ppermute x2, starting transfers between devices, swap(): lax.ppermute(first, axis, pairs)  4.32 us
    ppermute x2, waiting for transfers between devices, swap(): lax.ppermute(second, axis, others)  4.01 us
    ppermute x2, waiting for transfers between devices, swap(): lax.ppermute(first, axis, pairs)  2.87 us
  transfers between devices with their start and end apart: 6, of which 4 were waited for; matrix products, arithmetic and copies ran while one was open for 0% of the time, Pallas kernels for 1%

profile of v5, /device:TPU:1, one launch (start us, length us, event | category | flops | bytes accessed | tf_op | source)
XLA Modules:
  0.0 115.6 jit_solution(10988008383355196737)
XLA Ops:
  0.0 0.0 copy-start
  0.0 0.0 copy-start.1
  0.0 0.0 copy-start.2
  0.0 0.0 copy-start.6
  0.0 0.0 copy-start.5
  0.0 0.6 pad_add_fusion.odd_ref
  0.7 0.0 copy-start.3
  0.7 5.1 %edges.1 = (bf16[16,4096]{1,0:T(8,128)(2,1)}, bf16[16,4096]{1,0:T(8,128)(2,1)}, bf16[64,4096]{1,0:T(8,128)(2,1)}, bf16[64,4096]{1,0:T(8,128)(2,1)}) custom-call(s32[2]{0:T(128)} %pad_add_fusion.odd_ref, bf16[2,32,256]{2,1,0:T(8,128)(2,1)} %constant.34.clone.pick_ref, bf16[64,16,4096]{2,1,0:T(8,128)(2,1)} %after_ref.1), custom_call_target="tpu_custom_call" | custom-call | tf_op jit(solution)/shard_map/edges/pallas_call | solution.py:275
  5.8 3.2 %collective-permute-start.2 = (bf16[64,4096]{1,0:T(8,128)(2,1)}, bf16[64,4096]{1,0:T(8,128)(2,1)S(1)}, u32[]{:S(2)}, u32[]{:S(2)}) collective-permute-start(bf16[64,4096]{1,0:T(8,128)(2,1)} %get-tuple-element.15), channel_id=1, source_target_pairs={{0,16},{16,0},{32,48},{48,32},{64,80},{80,64},{96,112},{112,96},{1... | collective-permute-start | bytes 1572872 | tf_op jit(solution)/shard_map/ppermute | solution.py:339
  9.0 1.9 %collective-permute-start.3 = (bf16[64,4096]{1,0:T(8,128)(2,1)}, bf16[64,4096]{1,0:T(8,128)(2,1)S(1)}, u32[]{:S(2)}, u32[]{:S(2)}) collective-permute-start(bf16[64,4096]{1,0:T(8,128)(2,1)} %get-tuple-element.16), channel_id=1, source_target_pairs={{16,32},{32,16},{48,64},{64,48},{80,96},{96,80},{112,128},{128,112... | collective-permute-start | bytes 1572872 | tf_op jit(solution)/shard_map/ppermute | solution.py:339
  10.9 1.1 collective-permute-start
  12.0 0.0 copy-start.4
  12.0 0.8 collective-permute-start.1
  12.8 2.9 %collective-permute-done.za_ref = bf16[16,4096]{1,0:T(8,128)(2,1)S(1)} collective-permute-done((bf16[16,4096]{1,0:T(8,128)(2,1)}, bf16[16,4096]{1,0:T(8,128)(2,1)S(1)}, u32[]{:S(2)}, u32[]{:S(2)}) %collective-permute-start) | collective-permute-done | bytes 131104 | tf_op jit(solution)/shard_map/ppermute | solution.py:339
  15.7 0.0 collective-permute-done.1.zb_ref
  15.7 0.0 collective-permute-done.2.ya_ref.yan_ref
  15.7 4.0 %collective-permute-done.3.yb_ref.ybn_ref = bf16[64,4096]{1,0:T(8,128)(2,1)S(1)} collective-permute-done((bf16[64,4096]{1,0:T(8,128)(2,1)}, bf16[64,4096]{1,0:T(8,128)(2,1)S(1)}, u32[]{:S(2)}, u32[]{:S(2)}) %collective-permute-start.3) | collective-permute-done | bytes 524320 | tf_op jit(solution)/shard_map/ppermute | solution.py:339
  19.7 0.0 copy-done
  19.7 0.0 copy-done.1
  19.7 0.0 copy-done.2
  19.7 0.0 copy-done.6
  19.7 0.0 copy-done.5
  19.7 0.0 copy-done.3
  19.8 42.0 %march.1 = (f32[16,4,16,256]{3,2,1,0:T(8,128)}, f32[16,3,16,256]{3,2,1,0:T(8,128)S(1)}) custom-call(s32[2]{0:T(128)S(1)} %copy-done.3, f32[3]{0:T(128)S(1)} %copy-done.5, f32[3,16]{1,0:T(4,128)S(1)} %copy-done.2, f32[16]{0:T(128)S(1)} %copy-done.6, bf16[3,512,256]{2,1,0:T(8,128)(2,1)S(1)} %copy-done, bf16[3,512,256]{2,1,0:T(8,128)(2,1)S(1)} %copy-done, ...), custom_call_target="tpu_custom_call" | custom-call | flops 400000000 | bytes 24000000 | tf_op jit(solution)/shard_map/march/pallas_call | solution.py:216
  61.8 2.2 %convert_element_type.16 = f16[16,4,16,256]{3,2,1,0:T(8,128)(2,1)} convert(f32[16,4,16,256]{3,2,1,0:T(8,128)} %get-tuple-element.18) | non-fusion elementwise | flops 262144 | bytes 1572864 | tf_op jit(solution)/shard_map/convert_element_type | solution.py:355
  63.9 6.3 %all-to-all-start = ((f16[16,4,16,256]{3,2,1,0:T(8,128)(2,1)}), f16[16,4,16,256]{3,2,1,0:T(8,128)(2,1)S(1)}, u32[]{:S(2)}, u32[]{:S(2)}) async-start(f16[16,4,16,256]{3,2,1,0:T(8,128)(2,1)} %convert_element_type.16), calls=%async_computation | async-start | bytes 1048576 | tf_op jit(solution)/shard_map/all_to_all | solution.py:343
  70.9 0.1 convert.7
  71.0 10.5 %all-to-all-done = f16[16,4,16,256]{3,2,1,0:T(8,128)(2,1)S(1)} async-done(((f16[16,4,16,256]{3,2,1,0:T(8,128)(2,1)}), f16[16,4,16,256]{3,2,1,0:T(8,128)(2,1)S(1)}, u32[]{:S(2)}, u32[]{:S(2)}) %all-to-all-start) | async-done | bytes 524320 | tf_op jit(solution)/shard_map/all_to_all | solution.py:343
  81.5 0.1 convert_element_type.17.s_ref.f_ref
  81.6 0.0 copy-done.4
  81.6 0.7 front.1
  82.3 0.1 pad_maximum_fusion
  82.5 13.2 %all_to_all.15 = f16[16,4,16,256]{3,2,1,0:T(8,128)(2,1)S(1)} all-to-all(f16[16,4,16,256]{3,2,1,0:T(8,128)(2,1)S(1)} %pad_maximum_fusion), channel_id=1, replica_groups=mesh['tile'=16,'depth'=16] {'depth'}, dimensions={0} | all-to-all | bytes 1048576 | tf_op jit(solution)/shard_map/all_to_all | solution.py:343
  95.7 0.6 broadcast_in_dim.7
  96.4 10.6 %all-to-all-start.2 = ((f32[16,8,128]{2,1,0:T(8,128)}), f32[16,8,128]{2,1,0:T(8,128)S(1)}, u32[]{:S(2)}, u32[]{:S(2)}) async-start(f32[16,8,128]{2,1,0:T(8,128)} %broadcast_in_dim.7), calls=%async_computation.2 | async-start | bytes 131072 | tf_op jit(solution)/shard_map/all_to_all | solution.py:343
  107.0 0.1 slice_convert_fusion.s_ref
  107.0 0.6 back.1.second_ref
  107.7 7.1 %all-to-all-done.2.lum_ref = f32[16,8,128]{2,1,0:T(8,128)S(1)} async-done(((f32[16,8,128]{2,1,0:T(8,128)}), f32[16,8,128]{2,1,0:T(8,128)S(1)}, u32[]{:S(2)}, u32[]{:S(2)}) %all-to-all-start.2) | async-done | bytes 65568 | tf_op jit(solution)/shard_map/all_to_all | solution.py:343
  114.8 0.8 finish.1
  (4 shorter events, 0.0 us)
Async XLA Ops:
  0.0 19.7 %copy-start = (bf16[3,512,256]{2,1,0:T(8,128)(2,1)S(1)}, bf16[3,512,256]{2,1,0:T(8,128)(2,1)}, u32[]{:S(2)}) copy-start(bf16[3,512,256]{2,1,0:T(8,128)(2,1)} %constant.35.clone.sxf_ref.sx_ref.sxl_ref) | copy-start | bytes 2359300
  0.0 19.7 %copy-start.1 = (bf16[2,2,128,256]{3,2,1,0:T(8,128)(2,1)S(1)}, bf16[2,2,128,256]{3,2,1,0:T(8,128)(2,1)}, u32[]{:S(2)}) copy-start(bf16[2,2,128,256]{3,2,1,0:T(8,128)(2,1)} %constant.36.clone.sy_ref) | copy-start | bytes 786436
  0.0 19.7 %copy-start.2 = (f32[3,16]{1,0:T(4,128)S(1)}, f32[3,16]{1,0:T(4,128)}, u32[]{:S(2)}) copy-start(f32[3,16]{1,0:T(4,128)} %color_ref.1) | copy-start | bytes 580
  0.0 19.7 %copy-start.6 = (f32[16]{0:T(128)S(1)}, f32[16]{0:T(128)}, u32[]{:S(2)}) copy-start(f32[16]{0:T(128)} %opacity_ref.1) | copy-start | bytes 196
  0.0 19.7 %copy-start.5 = (f32[3]{0:T(128)S(1)}, f32[3]{0:T(128)}, u32[]{:S(2)}) copy-start(f32[3]{0:T(128)} %light_ref.1) | copy-start | bytes 40
  0.7 19.1 %copy-start.3 = (s32[2]{0:T(128)S(1)}, s32[2]{0:T(128)}, u32[]{:S(2)}) copy-start(s32[2]{0:T(128)} %pad_add_fusion.odd_ref) | copy-start | bytes 28
  5.8 9.9 %collective-permute-start.2 = (bf16[64,4096]{1,0:T(8,128)(2,1)}, bf16[64,4096]{1,0:T(8,128)(2,1)S(1)}, u32[]{:S(2)}, u32[]{:S(2)}) collective-permute-start(bf16[64,4096]{1,0:T(8,128)(2,1)} %get-tuple-element.15), channel_id=1, source_target_pairs={{0,16},{16,0},{32,48},{48,32},{64,80},{80,64},{96,112},{112,96},{1... | collective-permute-start | bytes 1572872 | tf_op jit(solution)/shard_map/ppermute | solution.py:339
  9.0 10.7 %collective-permute-start.3 = (bf16[64,4096]{1,0:T(8,128)(2,1)}, bf16[64,4096]{1,0:T(8,128)(2,1)S(1)}, u32[]{:S(2)}, u32[]{:S(2)}) collective-permute-start(bf16[64,4096]{1,0:T(8,128)(2,1)} %get-tuple-element.16), channel_id=1, source_target_pairs={{16,32},{32,16},{48,64},{64,48},{80,96},{96,80},{112,128},{128,112... | collective-permute-start | bytes 1572872 | tf_op jit(solution)/shard_map/ppermute | solution.py:339
  10.9 4.8 %collective-permute-start = (bf16[16,4096]{1,0:T(8,128)(2,1)}, bf16[16,4096]{1,0:T(8,128)(2,1)S(1)}, u32[]{:S(2)}, u32[]{:S(2)}) collective-permute-start(bf16[16,4096]{1,0:T(8,128)(2,1)} %get-tuple-element.13), channel_id=1, source_target_pairs={{0,1},{1,0},{2,3},{3,2},{4,5},{5,4},{6,7},{7,6},{8,9},{9,8},{10,11... | collective-permute-start | bytes 393224 | tf_op jit(solution)/shard_map/ppermute | solution.py:339
  12.0 69.6 %copy-start.4 = (f32[3]{0:T(128)S(1)}, f32[3]{0:T(128)}, u32[]{:S(2)}) copy-start(f32[3]{0:T(128)} %bg_ref.3) | copy-start | bytes 40
  12.0 3.7 %collective-permute-start.1 = (bf16[16,4096]{1,0:T(8,128)(2,1)}, bf16[16,4096]{1,0:T(8,128)(2,1)S(1)}, u32[]{:S(2)}, u32[]{:S(2)}) collective-permute-start(bf16[16,4096]{1,0:T(8,128)(2,1)} %get-tuple-element.14), channel_id=1, source_target_pairs={{1,2},{2,1},{3,4},{4,3},{5,6},{6,5},{7,8},{8,7},{9,10},{10,9},{11,... | collective-permute-start | bytes 393224 | tf_op jit(solution)/shard_map/ppermute | solution.py:339
  63.9 17.6 %all-to-all-start = ((f16[16,4,16,256]{3,2,1,0:T(8,128)(2,1)}), f16[16,4,16,256]{3,2,1,0:T(8,128)(2,1)S(1)}, u32[]{:S(2)}, u32[]{:S(2)}) async-start(f16[16,4,16,256]{3,2,1,0:T(8,128)(2,1)} %convert_element_type.16), calls=%async_computation | async-start | bytes 1048576 | tf_op jit(solution)/shard_map/all_to_all | solution.py:343
  96.4 18.4 %all-to-all-start.2 = ((f32[16,8,128]{2,1,0:T(8,128)}), f32[16,8,128]{2,1,0:T(8,128)S(1)}, u32[]{:S(2)}, u32[]{:S(2)}) async-start(f32[16,8,128]{2,1,0:T(8,128)} %broadcast_in_dim.7), calls=%async_computation.2 | async-start | bytes 131072 | tf_op jit(solution)/shard_map/all_to_all | solution.py:343

commit v6 on v5

--- a/solution.py
+++ b/solution.py
@@ -27,7 +27,7 @@
 DEPTH = 16
 WIDE = 256
 KNOTS = 16
-VMEM = 50 * 1024 * 1024
+VMEM = 44 * 1024 * 1024
 SMALL = 16 * 1024 * 1024
 
 

time: 116 us -> 114 us (0.983)
  other arithmetic: 3.23 us -> 1.96 us
    convert_element_type x2, other arithmetic: 2.31 us -> 1.04 us  [local(): front = exchange(front.astype(f16), 'depth').astype(f32)]
where the time goes in v6:
time: 114 us
  Pallas kernels  48.6 us (43%)
  waiting for transfers between devices  24.5 us (21%)
  starting transfers between devices  23.9 us (21%)
  blocking collectives  13.2 us (12%)
  other arithmetic  1.96 us (2%)
    pallas_call x1, Pallas kernels, march(): pl.pallas_call(march_kernel, grid=(steps,), in_specs=[smem, smem, smem, s...  41.4 us
    all_to_all x2, waiting for transfers between devices, exchange(): return lax.all_to_all(part, axis, split_axis=0, concat_axis=0, tiled=True)  17.6 us
    all_to_all x2, starting transfers between devices, exchange(): return lax.all_to_all(part, axis, split_axis=0, concat_axis=0, tiled=True)  16.9 us
    all_to_all x1, blocking collectives, exchange(): return lax.all_to_all(part, axis, split_axis=0, concat_axis=0, tiled=True)  13.2 us
    pallas_call x1, Pallas kernels, edges(): pl.pallas_call(edges_kernel, grid=(vol.shape[2] // width,), in_specs=[pl....  5.13 us
    ppermute x2, starting transfers between devices, swap(): lax.ppermute(first, axis, pairs)  4.32 us
    ppermute x2, waiting for transfers between devices, swap(): lax.ppermute(second, axis, others)  4.01 us
    ppermute x2, waiting for transfers between devices, swap(): lax.ppermute(first, axis, pairs)  2.87 us
  transfers between devices with their start and end apart: 6, of which 4 were waited for; matrix products, arithmetic and copies ran while one was open for 0% of the time, Pallas kernels for 1%

profile of v6, /device:TPU:1, one launch (start us, length us, event | category | flops | bytes accessed | tf_op | source)
XLA Modules:
  0.0 113.7 jit_solution(18133266837871534849)
XLA Ops:
  0.0 0.0 copy-start
  0.0 0.0 copy-start.1
  0.0 0.0 copy-start.2
  0.0 0.0 copy-start.6
  0.0 0.0 copy-start.5
  0.0 0.6 pad_add_fusion.odd_ref
  0.7 0.0 copy-start.3
  0.7 5.1 %edges.1 = (bf16[16,4096]{1,0:T(8,128)(2,1)}, bf16[16,4096]{1,0:T(8,128)(2,1)}, bf16[64,4096]{1,0:T(8,128)(2,1)}, bf16[64,4096]{1,0:T(8,128)(2,1)}) custom-call(s32[2]{0:T(128)} %pad_add_fusion.odd_ref, bf16[2,32,256]{2,1,0:T(8,128)(2,1)} %constant.34.clone.pick_ref, bf16[64,16,4096]{2,1,0:T(8,128)(2,1)} %after_ref.1), custom_call_target="tpu_custom_call" | custom-call | tf_op jit(solution)/shard_map/edges/pallas_call | solution.py:275
  5.8 3.2 %collective-permute-start.2 = (bf16[64,4096]{1,0:T(8,128)(2,1)}, bf16[64,4096]{1,0:T(8,128)(2,1)S(1)}, u32[]{:S(2)}, u32[]{:S(2)}) collective-permute-start(bf16[64,4096]{1,0:T(8,128)(2,1)} %get-tuple-element.15), channel_id=1, source_target_pairs={{0,16},{16,0},{32,48},{48,32},{64,80},{80,64},{96,112},{112,96},{1... | collective-permute-start | bytes 1572872 | tf_op jit(solution)/shard_map/ppermute | solution.py:339
  9.0 1.9 %collective-permute-start.3 = (bf16[64,4096]{1,0:T(8,128)(2,1)}, bf16[64,4096]{1,0:T(8,128)(2,1)S(1)}, u32[]{:S(2)}, u32[]{:S(2)}) collective-permute-start(bf16[64,4096]{1,0:T(8,128)(2,1)} %get-tuple-element.16), channel_id=1, source_target_pairs={{16,32},{32,16},{48,64},{64,48},{80,96},{96,80},{112,128},{128,112... | collective-permute-start | bytes 1572872 | tf_op jit(solution)/shard_map/ppermute | solution.py:339
  10.9 1.1 collective-permute-start
  12.0 0.0 copy-start.4
  12.0 0.8 collective-permute-start.1
  12.8 2.9 %collective-permute-done.za_ref = bf16[16,4096]{1,0:T(8,128)(2,1)S(1)} collective-permute-done((bf16[16,4096]{1,0:T(8,128)(2,1)}, bf16[16,4096]{1,0:T(8,128)(2,1)S(1)}, u32[]{:S(2)}, u32[]{:S(2)}) %collective-permute-start) | collective-permute-done | bytes 131104 | tf_op jit(solution)/shard_map/ppermute | solution.py:339
  15.7 0.0 collective-permute-done.1.zb_ref
  15.7 0.0 collective-permute-done.2.ya_ref.yan_ref
  15.7 4.0 %collective-permute-done.3.yb_ref.ybn_ref = bf16[64,4096]{1,0:T(8,128)(2,1)S(1)} collective-permute-done((bf16[64,4096]{1,0:T(8,128)(2,1)}, bf16[64,4096]{1,0:T(8,128)(2,1)S(1)}, u32[]{:S(2)}, u32[]{:S(2)}) %collective-permute-start.3) | collective-permute-done | bytes 524320 | tf_op jit(solution)/shard_map/ppermute | solution.py:339
  19.7 0.0 copy-done
  19.7 0.0 copy-done.1
  19.7 0.0 copy-done.2
  19.7 0.0 copy-done.6
  19.7 0.0 copy-done.5
  19.7 0.0 copy-done.3
  19.8 41.4 %march.1 = (f32[16,4,16,256]{3,2,1,0:T(8,128)S(1)}, f32[16,3,16,256]{3,2,1,0:T(8,128)S(1)}) custom-call(s32[2]{0:T(128)S(1)} %copy-done.3, f32[3]{0:T(128)S(1)} %copy-done.5, f32[3,16]{1,0:T(4,128)S(1)} %copy-done.2, f32[16]{0:T(128)S(1)} %copy-done.6, bf16[3,512,256]{2,1,0:T(8,128)(2,1)S(1)} %copy-done, bf16[3,512,256]{2,1,0:T(8,128)(2,1)S(1)} %copy-done, ...), custom_call_target="tpu_custom_call" | custom-call | flops 400000000 | bytes 24000000 | tf_op jit(solution)/shard_map/march/pallas_call | solution.py:216
  61.2 0.9 convert_element_type.16
  62.1 6.3 %all-to-all-start = ((f16[16,4,16,256]{3,2,1,0:T(8,128)(2,1)}), f16[16,4,16,256]{3,2,1,0:T(8,128)(2,1)S(1)}, u32[]{:S(2)}, u32[]{:S(2)}) async-start(f16[16,4,16,256]{3,2,1,0:T(8,128)(2,1)} %convert_element_type.16), calls=%async_computation | async-start | bytes 1048576 | tf_op jit(solution)/shard_map/all_to_all | solution.py:343
  69.0 0.1 convert.7
  69.1 10.5 %all-to-all-done = f16[16,4,16,256]{3,2,1,0:T(8,128)(2,1)S(1)} async-done(((f16[16,4,16,256]{3,2,1,0:T(8,128)(2,1)}), f16[16,4,16,256]{3,2,1,0:T(8,128)(2,1)S(1)}, u32[]{:S(2)}, u32[]{:S(2)}) %all-to-all-start) | async-done | bytes 524320 | tf_op jit(solution)/shard_map/all_to_all | solution.py:343
  79.6 0.1 convert_element_type.17.s_ref.f_ref
  79.8 0.0 copy-done.4
  79.8 0.7 front.1
  80.5 0.1 pad_maximum_fusion
  80.6 13.2 %all_to_all.15 = f16[16,4,16,256]{3,2,1,0:T(8,128)(2,1)S(1)} all-to-all(f16[16,4,16,256]{3,2,1,0:T(8,128)(2,1)S(1)} %pad_maximum_fusion), channel_id=1, replica_groups=mesh['tile'=16,'depth'=16] {'depth'}, dimensions={0} | all-to-all | bytes 1048576 | tf_op jit(solution)/shard_map/all_to_all | solution.py:343
  93.8 0.6 broadcast_in_dim.7
  94.5 10.6 %all-to-all-start.2 = ((f32[16,8,128]{2,1,0:T(8,128)}), f32[16,8,128]{2,1,0:T(8,128)S(1)}, u32[]{:S(2)}, u32[]{:S(2)}) async-start(f32[16,8,128]{2,1,0:T(8,128)} %broadcast_in_dim.7), calls=%async_computation.2 | async-start | bytes 131072 | tf_op jit(solution)/shard_map/all_to_all | solution.py:343
  105.1 0.1 slice_convert_fusion.s_ref
  105.2 0.6 back.1.second_ref
  105.8 7.1 %all-to-all-done.2.lum_ref = f32[16,8,128]{2,1,0:T(8,128)S(1)} async-done(((f32[16,8,128]{2,1,0:T(8,128)}), f32[16,8,128]{2,1,0:T(8,128)S(1)}, u32[]{:S(2)}, u32[]{:S(2)}) %all-to-all-start.2) | async-done | bytes 65568 | tf_op jit(solution)/shard_map/all_to_all | solution.py:343
  112.9 0.8 finish.1
  (4 shorter events, 0.0 us)
Async XLA Ops:
  0.0 19.7 %copy-start = (bf16[3,512,256]{2,1,0:T(8,128)(2,1)S(1)}, bf16[3,512,256]{2,1,0:T(8,128)(2,1)}, u32[]{:S(2)}) copy-start(bf16[3,512,256]{2,1,0:T(8,128)(2,1)} %constant.35.clone.sxf_ref.sx_ref.sxl_ref) | copy-start | bytes 2359300
  0.0 19.7 %copy-start.1 = (bf16[2,2,128,256]{3,2,1,0:T(8,128)(2,1)S(1)}, bf16[2,2,128,256]{3,2,1,0:T(8,128)(2,1)}, u32[]{:S(2)}) copy-start(bf16[2,2,128,256]{3,2,1,0:T(8,128)(2,1)} %constant.36.clone.sy_ref) | copy-start | bytes 786436
  0.0 19.7 %copy-start.2 = (f32[3,16]{1,0:T(4,128)S(1)}, f32[3,16]{1,0:T(4,128)}, u32[]{:S(2)}) copy-start(f32[3,16]{1,0:T(4,128)} %color_ref.1) | copy-start | bytes 580
  0.0 19.7 %copy-start.6 = (f32[16]{0:T(128)S(1)}, f32[16]{0:T(128)}, u32[]{:S(2)}) copy-start(f32[16]{0:T(128)} %opacity_ref.1) | copy-start | bytes 196
  0.0 19.7 %copy-start.5 = (f32[3]{0:T(128)S(1)}, f32[3]{0:T(128)}, u32[]{:S(2)}) copy-start(f32[3]{0:T(128)} %light_ref.1) | copy-start | bytes 40
  0.7 19.1 %copy-start.3 = (s32[2]{0:T(128)S(1)}, s32[2]{0:T(128)}, u32[]{:S(2)}) copy-start(s32[2]{0:T(128)} %pad_add_fusion.odd_ref) | copy-start | bytes 28
  5.8 9.9 %collective-permute-start.2 = (bf16[64,4096]{1,0:T(8,128)(2,1)}, bf16[64,4096]{1,0:T(8,128)(2,1)S(1)}, u32[]{:S(2)}, u32[]{:S(2)}) collective-permute-start(bf16[64,4096]{1,0:T(8,128)(2,1)} %get-tuple-element.15), channel_id=1, source_target_pairs={{0,16},{16,0},{32,48},{48,32},{64,80},{80,64},{96,112},{112,96},{1... | collective-permute-start | bytes 1572872 | tf_op jit(solution)/shard_map/ppermute | solution.py:339
  9.0 10.7 %collective-permute-start.3 = (bf16[64,4096]{1,0:T(8,128)(2,1)}, bf16[64,4096]{1,0:T(8,128)(2,1)S(1)}, u32[]{:S(2)}, u32[]{:S(2)}) collective-permute-start(bf16[64,4096]{1,0:T(8,128)(2,1)} %get-tuple-element.16), channel_id=1, source_target_pairs={{16,32},{32,16},{48,64},{64,48},{80,96},{96,80},{112,128},{128,112... | collective-permute-start | bytes 1572872 | tf_op jit(solution)/shard_map/ppermute | solution.py:339
  10.9 4.8 %collective-permute-start = (bf16[16,4096]{1,0:T(8,128)(2,1)}, bf16[16,4096]{1,0:T(8,128)(2,1)S(1)}, u32[]{:S(2)}, u32[]{:S(2)}) collective-permute-start(bf16[16,4096]{1,0:T(8,128)(2,1)} %get-tuple-element.13), channel_id=1, source_target_pairs={{0,1},{1,0},{2,3},{3,2},{4,5},{5,4},{6,7},{7,6},{8,9},{9,8},{10,11... | collective-permute-start | bytes 393224 | tf_op jit(solution)/shard_map/ppermute | solution.py:339
  12.0 67.7 %copy-start.4 = (f32[3]{0:T(128)S(1)}, f32[3]{0:T(128)}, u32[]{:S(2)}) copy-start(f32[3]{0:T(128)} %bg_ref.3) | copy-start | bytes 40
  12.0 3.7 %collective-permute-start.1 = (bf16[16,4096]{1,0:T(8,128)(2,1)}, bf16[16,4096]{1,0:T(8,128)(2,1)S(1)}, u32[]{:S(2)}, u32[]{:S(2)}) collective-permute-start(bf16[16,4096]{1,0:T(8,128)(2,1)} %get-tuple-element.14), channel_id=1, source_target_pairs={{1,2},{2,1},{3,4},{4,3},{5,6},{6,5},{7,8},{8,7},{9,10},{10,9},{11,... | collective-permute-start | bytes 393224 | tf_op jit(solution)/shard_map/ppermute | solution.py:339
  62.1 17.6 %all-to-all-start = ((f16[16,4,16,256]{3,2,1,0:T(8,128)(2,1)}), f16[16,4,16,256]{3,2,1,0:T(8,128)(2,1)S(1)}, u32[]{:S(2)}, u32[]{:S(2)}) async-start(f16[16,4,16,256]{3,2,1,0:T(8,128)(2,1)} %convert_element_type.16), calls=%async_computation | async-start | bytes 1048576 | tf_op jit(solution)/shard_map/all_to_all | solution.py:343
  94.5 18.4 %all-to-all-start.2 = ((f32[16,8,128]{2,1,0:T(8,128)}), f32[16,8,128]{2,1,0:T(8,128)S(1)}, u32[]{:S(2)}, u32[]{:S(2)}) async-start(f32[16,8,128]{2,1,0:T(8,128)} %broadcast_in_dim.7), calls=%async_computation.2 | async-start | bytes 131072 | tf_op jit(solution)/shard_map/all_to_all | solution.py:343
